TPU v7x, 512 devices: a whole 4x4x16 slice. The times are simulated.
512 devices in a mesh: dp: 32 (over x_lo, z), seq: 16 (over x_hi, y, core).
Axes of the slice: x: 4 (x_hi: 2, x_lo: 2; x = x_hi * 2 + x_lo), y: 4, z: 16, core: 2. Of those that a mesh axis runs over, the one named last changes fastest.
Arguments:
- q_raw: bfloat16 [32, 2048, 2048], P('dp', 'seq'), may hold values from -6 to 6
- key_unnormed: bfloat16 [32, 2048, 1024], P('dp', 'seq'), may hold values from -6 to 6
- value_input: bfloat16 [32, 2048, 1024], P('dp', 'seq'), may hold values from -24 to 24
- grad_attended: bfloat16 [32, 2048, 2048], P('dp', 'seq'), may hold values from -48 to 48
- segment_ids: int32 [32, 2048], P('dp', 'seq'), may hold values from 0 to 3, never falling along the last dimension, each value on 1 to 1024 neighbouring positions
- q_gain: float32 [128], replicated, may hold values from 0.1 to 1.9
- key_norm_gain: float32 [128], replicated, may hold values from 0.1 to 1.9
Outputs:
- attended: bfloat16 [32, 2048, 2048], P('dp', 'seq')
- grad_q: bfloat16 [32, 2048, 2048], P('dp', 'seq')
- grad_k: bfloat16 [32, 2048, 1024], P('dp', 'seq')
- grad_value: bfloat16 [32, 2048, 1024], P('dp', 'seq')
- grad_q_gain: float32 [128], replicated
- key_gain_gradient: float32 [128], replicated
Inputs may be any that keep to these rules, and one draw needn't show every extreme that they name: `segment_ids`: within a trajectory the numbers never fall; every document number appears, a document holds at most 1024 tokens, and one holds exactly that many.
All inputs are finite; a program needn't handle non-finite values.
Results may differ from a plain program's by a relative error of at most 0.0085.
Values may be sent and summed in bfloat16 or wider, within the bound.
A program may use at most 64 MiB of HBM per device.

v0:
```python
import math

import jax
import jax.numpy as jnp
from jax import lax
from jax.sharding import PartitionSpec as P

EPSILON = 1e-06
BLOCK_LIMIT = 512


def unit_components(vectors, gain_vec):
    vectors = vectors.astype(jnp.float32)
    inverse = lax.rsqrt(jnp.mean(vectors * vectors, axis=-1, keepdims=True) + EPSILON)
    unit_rows = vectors * inverse
    return (inverse, unit_rows, (unit_rows * gain_vec).astype(jnp.bfloat16))


def norm_backward_pass(gradient, inverse, unit_rows, gain_vec):
    scaled = gradient * gain_vec
    centred = scaled - unit_rows * jnp.mean(scaled * unit_rows, axis=-1, keepdims=True)
    return (inverse * centred).astype(jnp.bfloat16)


def shards(q_raw, key_unnormed, value_input, grad_attended, segment_ids, q_gain, key_norm_gain):
    tok_rows = q_raw.shape[1]
    seq_ways = lax.axis_size("seq")
    head_dim = q_gain.shape[0]
    q_heads = q_raw.shape[2] // head_dim
    kv_heads = key_unnormed.shape[2] // head_dim
    group_width = q_heads // kv_heads
    local_q = q_heads // seq_ways
    sequence_length = tok_rows * seq_ways
    q_inv, q_unit, query_gain_scaled = unit_components(
        q_raw[0].reshape(tok_rows, q_heads, head_dim), q_gain
    )
    key_inverse_norm, key_unit_length, key_gain_scaled = unit_components(
        key_unnormed[0].reshape(tok_rows, kv_heads, head_dim), key_norm_gain
    )
    values = value_input[0].reshape(tok_rows, kv_heads, head_dim)
    segment_all = lax.all_gather(segment_ids[0], "seq", axis=0, tiled=True)
    g_send = grad_attended[0].reshape(tok_rows, seq_ways, local_q * head_dim)
    k_send = jnp.repeat(key_gain_scaled, group_width, axis=1)
    v_send = jnp.repeat(values, group_width, axis=1)
    q_here, g_here, k_here, v_here = (
        lax.all_to_all(query_gain_scaled, "seq", split_axis=1, concat_axis=0, tiled=True),
        lax.all_to_all(g_send, "seq", split_axis=1, concat_axis=0, tiled=True),
        lax.all_to_all(k_send, "seq", split_axis=1, concat_axis=0, tiled=True),
        lax.all_to_all(v_send, "seq", split_axis=1, concat_axis=0, tiled=True),
    )
    block_rows = min(BLOCK_LIMIT, sequence_length)
    score_scale = head_dim ** (-0.5)
    key_positions = jnp.arange(sequence_length, dtype=jnp.int32)

    def block_step(block_index, loop_state):
        attended, grad_query, key_gradient, value_gradient = loop_state
        row_start = block_index * block_rows
        q_block = lax.dynamic_slice_in_dim(q_here, row_start, block_rows, 0)
        g_block = lax.dynamic_slice_in_dim(g_here, row_start, block_rows, 0)
        segment_block = lax.dynamic_slice_in_dim(segment_all, row_start, block_rows, 0)
        query_positions = row_start + jnp.arange(block_rows, dtype=jnp.int32)
        allowed = (key_positions[None, :] <= query_positions[:, None]) & (
            segment_all[None, :] == segment_block[:, None]
        )
        scores = (
            jnp.einsum("qhd,khd->hqk", q_block, k_here, preferred_element_type=jnp.float32)
            * score_scale
        )
        exp_scores = jnp.where(allowed[None], jnp.exp(scores), 0.0)
        weights = exp_scores / jnp.sum(exp_scores, axis=-1, keepdims=True)
        weights_b = weights.astype(jnp.bfloat16)
        out_block = jnp.einsum(
            "hqk,khd->qhd", weights_b, v_here, preferred_element_type=jnp.float32
        ).astype(jnp.bfloat16)
        grad_weights = jnp.einsum(
            "qhd,khd->hqk", g_block, v_here, preferred_element_type=jnp.float32
        )
        row_term = jnp.sum(weights * grad_weights, axis=-1, keepdims=True)
        grad_scores = (weights * (grad_weights - row_term) * score_scale).astype(jnp.bfloat16)
        query_block = jnp.einsum(
            "hqk,khd->qhd", grad_scores, k_here, preferred_element_type=jnp.float32
        )
        key_gradient = key_gradient + jnp.einsum(
            "hqk,qhd->khd", grad_scores, q_block, preferred_element_type=jnp.float32
        )
        value_gradient = value_gradient + jnp.einsum(
            "hqk,qhd->khd", weights_b, g_block, preferred_element_type=jnp.float32
        )
        attended = lax.dynamic_update_slice_in_dim(attended, out_block, row_start, 0)
        grad_query = lax.dynamic_update_slice_in_dim(grad_query, query_block, row_start, 0)
        return (attended, grad_query, key_gradient, value_gradient)

    zeros_float = jnp.zeros((sequence_length, local_q, head_dim), jnp.float32)
    initial = (
        jnp.zeros((sequence_length, local_q, head_dim), jnp.bfloat16),
        zeros_float,
        zeros_float,
        zeros_float,
    )
    attended, grad_query, key_gradient, value_gradient = lax.fori_loop(
        0, sequence_length // block_rows, block_step, initial
    )
    attended_back = lax.all_to_all(attended, "seq", split_axis=0, concat_axis=1, tiled=True)
    out_attended = attended_back.reshape(1, tok_rows, q_heads * head_dim)
    query_back, key_back, val_back = (
        lax.all_to_all(grad_query, "seq", split_axis=0, concat_axis=1, tiled=True),
        lax.all_to_all(key_gradient, "seq", split_axis=0, concat_axis=1, tiled=True),
        lax.all_to_all(value_gradient, "seq", split_axis=0, concat_axis=1, tiled=True),
    )
    key_tokens = key_back.reshape(tok_rows, kv_heads, group_width, head_dim).sum(axis=2)
    val_tokens = val_back.reshape(tok_rows, kv_heads, group_width, head_dim).sum(axis=2)
    out_q = norm_backward_pass(query_back, q_inv, q_unit, q_gain).reshape(
        1, tok_rows, q_heads * head_dim
    )
    output_key = norm_backward_pass(
        key_tokens, key_inverse_norm, key_unit_length, key_norm_gain
    ).reshape(1, tok_rows, kv_heads * head_dim)
    out_value = val_tokens.astype(jnp.bfloat16).reshape(1, tok_rows, kv_heads * head_dim)
    part_q = jnp.sum(query_back * q_unit, axis=(0, 1))
    key_portion = jnp.sum(key_tokens * key_unit_length, axis=(0, 1))
    total_q, total_k = lax.psum((part_q, key_portion), ("dp", "seq"))
    token_total = lax.axis_size("dp") * sequence_length
    grad_q_gain = total_q / math.sqrt(token_total * q_heads)
    key_gain_gradient = total_k / math.sqrt(token_total * kv_heads)
    return (out_attended, out_q, output_key, out_value, grad_q_gain, key_gain_gradient)


def solution(mesh):
    in_specs = (
        P("dp", "seq", None),
        P("dp", "seq", None),
        P("dp", "seq", None),
        P("dp", "seq", None),
        P("dp", "seq"),
        P(),
        P(),
    )
    out_specs = (
        P("dp", "seq", None),
        P("dp", "seq", None),
        P("dp", "seq", None),
        P("dp", "seq", None),
        P(),
        P(),
    )
    return jax.shard_map(shards, mesh=mesh, in_specs=in_specs, out_specs=out_specs, check_vma=False)
```

profile of v0, /device:TPU:1, one launch (start us, length us, event | category | flops | bytes accessed | tf_op | source)
XLA Modules:
  0.0 342.0 jit_solution(12555684011138797788)
XLA Ops:
  4.8 10.4 %all-to-all-start = ((bf16[128,16,128]{0,2,1:T(8,128)(2,1)}), bf16[128,16,128]{0,2,1:T(8,128)(2,1)S(1)}, u32[]{:S(2)}, u32[]{:S(2)}) async-start(bf16[128,16,128]{0,2,1:T(8,128)(2,1)} %multiply_convert_fusion.1), calls=%async_computation | async-start | bytes 1048576 | tf_op jit(solution)/shard_map/all_to_all | solution.py:46
  16.8 9.7 %all-to-all-done = bf16[128,16,128]{0,2,1:T(8,128)(2,1)S(1)} async-done(((bf16[128,16,128]{0,2,1:T(8,128)(2,1)}), bf16[128,16,128]{0,2,1:T(8,128)(2,1)S(1)}, u32[]{:S(2)}, u32[]{:S(2)}) %all-to-all-start) | async-done | bytes 524320 | tf_op jit(solution)/shard_map/all_to_all | solution.py:46
  27.4 4.5 %all-to-all-start.1 = ((bf16[128,16,128]{2,0,1:T(8,128)(2,1)}), bf16[128,16,128]{2,0,1:T(8,128)(2,1)S(1)}, u32[]{:S(2)}, u32[]{:S(2)}) async-start(bf16[128,16,128]{2,0,1:T(8,128)(2,1)} %bitcast.6), calls=%async_computation.1 | async-start | bytes 1048576 | tf_op jit(solution)/shard_map/all_to_all | solution.py:48
  33.0 10.4 %all-to-all-done.1 = bf16[128,16,128]{2,0,1:T(8,128)(2,1)S(1)} async-done(((bf16[128,16,128]{2,0,1:T(8,128)(2,1)}), bf16[128,16,128]{2,0,1:T(8,128)(2,1)S(1)}, u32[]{:S(2)}, u32[]{:S(2)}) %all-to-all-start.1) | async-done | bytes 524320 | tf_op jit(solution)/shard_map/all_to_all | solution.py:48
  43.4 4.5 %all-to-all-start.3 = ((bf16[128,16,128]{0,2,1:T(8,128)(2,1)}), bf16[128,16,128]{0,2,1:T(8,128)(2,1)S(1)}, u32[]{:S(2)}, u32[]{:S(2)}) async-start(bf16[128,16,128]{0,2,1:T(8,128)(2,1)} %bitcast.14), calls=%async_computation.3 | async-start | bytes 1048576 | tf_op jit(solution)/shard_map/all_to_all | solution.py:47
  48.0 11.3 %all-to-all-done.3 = bf16[128,16,128]{0,2,1:T(8,128)(2,1)S(1)} async-done(((bf16[128,16,128]{0,2,1:T(8,128)(2,1)}), bf16[128,16,128]{0,2,1:T(8,128)(2,1)S(1)}, u32[]{:S(2)}, u32[]{:S(2)}) %all-to-all-start.3) | async-done | bytes 524320 | tf_op jit(solution)/shard_map/all_to_all | solution.py:47
  60.2 5.1 %all-to-all-start.2 = ((bf16[128,16,128]{2,0,1:T(8,128)(2,1)}), bf16[128,16,128]{2,0,1:T(8,128)(2,1)}, u32[]{:S(2)}, u32[]{:S(2)}) async-start(bf16[128,16,128]{2,0,1:T(8,128)(2,1)} %bitcast.10), calls=%async_computation.2 | async-start | bytes 1048576 | tf_op jit(solution)/shard_map/all_to_all | solution.py:49
  65.3 24.3 %all-gather = s32[1,2048]{1,0:T(1,128)S(1)} all-gather(s32[1,128]{1,0:T(1,128)S(1)} %copy-done.22), channel_id=2, replica_groups=mesh['dp'=32,'seq'=16] {'seq'}, dimensions={1}, use_global_device_ids=true | all-gather | bytes 8704 | tf_op jit(solution)/shard_map/all_gather | solution.py:41
  92.2 56.1 %while.20 = (s32[]{:T(128)}, bf16[2048,1,128]{2,0,1:T(8,128)(2,1)}, f32[2048,1,128]{2,0,1:T(8,128)}, f32[2048,1,128]{0,2,1:T(8,128)S(1)}, f32[2048,1,128]{0,2,1:...) while((s32[]{:T(128)}, bf16[2048,1,128]{2,0,1:T(8,128)(2,1)}, ...), condition=%wide.region_5.6_spmd.clone, body=%wide.region_2.5_spmd.clone.sunk | while | flops 1630600704 | bytes 97419776 | solution.py:100
  93.8 2.3 multiply_reduce_fusion.4
  98.6 2.5 fusion.64
  103.6 2.6 fusion.63
  107.8 2.3 multiply_reduce_fusion.4
  112.6 2.5 fusion.64
  117.6 2.6 fusion.63
  121.9 2.3 multiply_reduce_fusion.4
  126.6 2.5 fusion.64
  131.7 2.6 fusion.63
  135.9 2.3 multiply_reduce_fusion.4
  140.7 2.4 fusion.64
  145.7 2.6 fusion.63
  148.8 2.1 reduce.12
  151.8 4.1 %all-to-all-start.4 = ((bf16[16,2,8192]{2,1,0:T(2,128)(2,1)}), bf16[16,2,8192]{2,1,0:T(2,128)(2,1)S(1)}, u32[]{:S(2)}, u32[]{:S(2)}) async-start(bf16[16,2,8192]{2,1,0:T(2,128)(2,1)} %reshape.261), calls=%async_computation.4 | async-start | bytes 1048576 | tf_op jit(solution)/shard_map/all_to_all | solution.py:103
  155.9 1.9 copy.113
  157.8 9.4 %all-to-all-done.4 = bf16[16,2,8192]{2,1,0:T(2,128)(2,1)S(1)} async-done(((bf16[16,2,8192]{2,1,0:T(2,128)(2,1)}), bf16[16,2,8192]{2,1,0:T(2,128)(2,1)S(1)}, u32[]{:S(2)}, u32[]{:S(2)}) %all-to-all-start.4) | async-done | bytes 524320 | tf_op jit(solution)/shard_map/all_to_all | solution.py:103
  167.2 21.6 %all_to_all.138 = f32[2048,1,128]{2,1,0:T(1,128)S(1)} all-to-all(f32[2048,1,128]{2,1,0:T(1,128)} %copy.113), channel_id=1, replica_groups=mesh['dp'=32,'seq'=16] {'seq'}, dimensions={0} | all-to-all | bytes 2097152 | tf_op jit(solution)/shard_map/all_to_all | solution.py:107
  188.8 4.6 %all-to-all-start.5 = ((f32[2048,1,128]{2,1,0:T(1,128)}), f32[2048,1,128]{2,1,0:T(1,128)S(1)}, u32[]{:S(2)}, u32[]{:S(2)}) async-start(f32[2048,1,128]{2,1,0:T(1,128)} %bitcast.206), calls=%async_computation.5 | async-start | bytes 2097152 | tf_op jit(solution)/shard_map/all_to_all | solution.py:106
  193.4 3.6 %copy.116 = f32[2048,1,128]{2,1,0:T(1,128)} copy(f32[2048,1,128]{0,2,1:T(8,128)} %get-tuple-element.196) | data formatting | bytes 2097152 | tf_op jit(solution)/shard_map/while | solution.py:100
  197.0 13.7 %all-to-all-done.5 = f32[2048,1,128]{2,1,0:T(1,128)S(1)} async-done(((f32[2048,1,128]{2,1,0:T(1,128)}), f32[2048,1,128]{2,1,0:T(1,128)S(1)}, u32[]{:S(2)}, u32[]{:S(2)}) %all-to-all-start.5) | async-done | bytes 1048608 | tf_op jit(solution)/shard_map/all_to_all | solution.py:106
  210.7 5.0 %all-to-all-start.7 = ((f32[2048,1,128]{2,1,0:T(1,128)}), f32[2048,1,128]{2,1,0:T(1,128)}, u32[]{:S(2)}, u32[]{:S(2)}) async-start(f32[2048,1,128]{2,1,0:T(1,128)} %copy.116), calls=%async_computation.7 | async-start | bytes 2097152 | tf_op jit(solution)/shard_map/all_to_all | solution.py:108
  226.7 6.4 %all-to-all-done.7 = f32[2048,1,128]{2,1,0:T(1,128)} async-done(((f32[2048,1,128]{2,1,0:T(1,128)}), f32[2048,1,128]{2,1,0:T(1,128)}, u32[]{:S(2)}, u32[]{:S(2)}) %all-to-all-start.7) | async-done | bytes 1048608 | tf_op jit(solution)/shard_map/all_to_all | solution.py:108
  235.5 106.0 %all-reduce = (f32[128]{0:T(128)S(1)}, f32[128]{0:T(128)S(1)}) all-reduce(f32[128]{0:T(128)S(1)} %get-tuple-element.268, f32[128]{0:T(128)S(1)} %bitcast_reduce_fusion), channel_id=1, replica_groups=mesh['dp'=32,'seq'=16] {'dp','seq'}, use_global_device_ids=true, to_apply=%region_11.12 | all-reduce | flops 256 | bytes 2048 | tf_op jit(solution)/shard_map/psum | solution.py:121
  (177 shorter events, 52.7 us)
Async XLA Ops:
  0.6 14.5 %copy-start.18 = (bf16[1,128,1024]{2,1,0:T(8,128)(2,1)S(1)}, bf16[1,128,1024]{2,1,0:T(8,128)(2,1)}, u32[]{:S(2)}) copy-start(bf16[1,128,1024]{2,1,0:T(8,128)(2,1)} %param.10) | copy-start | bytes 786436
  0.6 15.6 %copy-start.20 = (f32[128]{0:T(128)S(1)}, f32[128]{0:T(128)}, u32[]{:S(2)}) copy-start(f32[128]{0:T(128)} %param.15) | copy-start | bytes 1540
  2.0 25.4 %copy-start.6 = (bf16[1,128,2048]{1,2,0:T(8,128)(2,1)}, bf16[1,128,2048]{1,2,0:T(8,128)(2,1)S(1)}, u32[]{:S(2)}) copy-start(bf16[1,128,2048]{1,2,0:T(8,128)(2,1)S(1)} %copy.100) | copy-start | bytes 1572868
  2.0 30.0 %copy-start.15 = (bf16[1,128,2048]{2,1,0:T(8,128)(2,1)S(1)}, bf16[1,128,2048]{2,1,0:T(8,128)(2,1)}, u32[]{:S(2)}) copy-start(bf16[1,128,2048]{2,1,0:T(8,128)(2,1)} %param.12) | copy-start | bytes 1572868
  4.8 43.1 %copy-start.19 = (bf16[1,128,1024]{2,1,0:T(8,128)(2,1)S(1)}, bf16[1,128,1024]{2,1,0:T(8,128)(2,1)}, u32[]{:S(2)}) copy-start(bf16[1,128,1024]{2,1,0:T(8,128)(2,1)} %param.11) | copy-start | bytes 786436
  4.8 21.8 %all-to-all-start = ((bf16[128,16,128]{0,2,1:T(8,128)(2,1)}), bf16[128,16,128]{0,2,1:T(8,128)(2,1)S(1)}, u32[]{:S(2)}, u32[]{:S(2)}) async-start(bf16[128,16,128]{0,2,1:T(8,128)(2,1)} %multiply_convert_fusion.1), calls=%async_computation | async-start | bytes 1048576 | tf_op jit(solution)/shard_map/all_to_all | solution.py:46
  15.4 49.9 %copy-start.22 = (s32[1,128]{1,0:T(1,128)S(1)}, s32[1,128]{1,0:T(1,128)}, u32[]{:S(2)}) copy-start(s32[1,128]{1,0:T(1,128)} %param.13) | copy-start | bytes 1540
  27.4 15.9 %all-to-all-start.1 = ((bf16[128,16,128]{2,0,1:T(8,128)(2,1)}), bf16[128,16,128]{2,0,1:T(8,128)(2,1)S(1)}, u32[]{:S(2)}, u32[]{:S(2)}) async-start(bf16[128,16,128]{2,0,1:T(8,128)(2,1)} %bitcast.6), calls=%async_computation.1 | async-start | bytes 1048576 | tf_op jit(solution)/shard_map/all_to_all | solution.py:48
  43.4 15.9 %all-to-all-start.3 = ((bf16[128,16,128]{0,2,1:T(8,128)(2,1)}), bf16[128,16,128]{0,2,1:T(8,128)(2,1)S(1)}, u32[]{:S(2)}, u32[]{:S(2)}) async-start(bf16[128,16,128]{0,2,1:T(8,128)(2,1)} %bitcast.14), calls=%async_computation.3 | async-start | bytes 1048576 | tf_op jit(solution)/shard_map/all_to_all | solution.py:47
  60.2 30.1 %all-to-all-start.2 = ((bf16[128,16,128]{2,0,1:T(8,128)(2,1)}), bf16[128,16,128]{2,0,1:T(8,128)(2,1)}, u32[]{:S(2)}, u32[]{:S(2)}) async-start(bf16[128,16,128]{2,0,1:T(8,128)(2,1)} %bitcast.10), calls=%async_computation.2 | async-start | bytes 1048576 | tf_op jit(solution)/shard_map/all_to_all | solution.py:49
  96.9 4.1 %copy-start.1 = (f32[512,2048]{1,0:T(8,128)S(1)}, f32[512,2048]{1,0:T(8,128)}, u32[]{:S(2)}) copy-start(f32[512,2048]{1,0:T(8,128)} %copy-done) | copy-start | bytes 12582916 | tf_op jit(solution)/shard_map/while
  96.9 4.1 %copy-start.13 = (f32[2048,1,128]{0,2,1:T(8,128)S(1)}, f32[2048,1,128]{0,2,1:T(8,128)}, u32[]{:S(2)}) copy-start(f32[2048,1,128]{0,2,1:T(8,128)} %get-tuple-element.391) | copy-start | bytes 3145732 | tf_op jit(solution)/shard_map/while
  106.2 3.9 %copy-start.2 = (bf16[2048,1,128]{2,0,1:T(8,128)(2,1)}, bf16[2048,1,128]{2,0,1:T(8,128)(2,1)S(1)}, u32[]{:S(2)}) copy-start(bf16[2048,1,128]{2,0,1:T(8,128)(2,1)S(1)} %get-tuple-element.408) | copy-start | bytes 1572868 | tf_op jit(solution)/shard_map/while
  111.0 4.1 %copy-start.1 = (f32[512,2048]{1,0:T(8,128)S(1)}, f32[512,2048]{1,0:T(8,128)}, u32[]{:S(2)}) copy-start(f32[512,2048]{1,0:T(8,128)} %copy-done) | copy-start | bytes 12582916 | tf_op jit(solution)/shard_map/while
  111.0 4.1 %copy-start.13 = (f32[2048,1,128]{0,2,1:T(8,128)S(1)}, f32[2048,1,128]{0,2,1:T(8,128)}, u32[]{:S(2)}) copy-start(f32[2048,1,128]{0,2,1:T(8,128)} %get-tuple-element.391) | copy-start | bytes 3145732 | tf_op jit(solution)/shard_map/while
  120.2 3.9 %copy-start.2 = (bf16[2048,1,128]{2,0,1:T(8,128)(2,1)}, bf16[2048,1,128]{2,0,1:T(8,128)(2,1)S(1)}, u32[]{:S(2)}) copy-start(bf16[2048,1,128]{2,0,1:T(8,128)(2,1)S(1)} %get-tuple-element.408) | copy-start | bytes 1572868 | tf_op jit(solution)/shard_map/while
  120.3 3.9 %copy-start.11 = (bf16[2048,1,128]{2,0,1:T(8,128)(2,1)}, bf16[2048,1,128]{2,0,1:T(8,128)(2,1)S(1)}, u32[]{:S(2)}) copy-start(bf16[2048,1,128]{2,0,1:T(8,128)(2,1)S(1)} %get-tuple-element.407) | copy-start | bytes 1572868 | tf_op jit(solution)/shard_map/while
  125.0 4.1 %copy-start.1 = (f32[512,2048]{1,0:T(8,128)S(1)}, f32[512,2048]{1,0:T(8,128)}, u32[]{:S(2)}) copy-start(f32[512,2048]{1,0:T(8,128)} %copy-done) | copy-start | bytes 12582916 | tf_op jit(solution)/shard_map/while
  125.0 4.1 %copy-start.13 = (f32[2048,1,128]{0,2,1:T(8,128)S(1)}, f32[2048,1,128]{0,2,1:T(8,128)}, u32[]{:S(2)}) copy-start(f32[2048,1,128]{0,2,1:T(8,128)} %get-tuple-element.391) | copy-start | bytes 3145732 | tf_op jit(solution)/shard_map/while
  134.3 3.9 %copy-start.2 = (bf16[2048,1,128]{2,0,1:T(8,128)(2,1)}, bf16[2048,1,128]{2,0,1:T(8,128)(2,1)S(1)}, u32[]{:S(2)}) copy-start(bf16[2048,1,128]{2,0,1:T(8,128)(2,1)S(1)} %get-tuple-element.408) | copy-start | bytes 1572868 | tf_op jit(solution)/shard_map/while
  134.3 3.9 %copy-start.11 = (bf16[2048,1,128]{2,0,1:T(8,128)(2,1)}, bf16[2048,1,128]{2,0,1:T(8,128)(2,1)S(1)}, u32[]{:S(2)}) copy-start(bf16[2048,1,128]{2,0,1:T(8,128)(2,1)S(1)} %get-tuple-element.407) | copy-start | bytes 1572868 | tf_op jit(solution)/shard_map/while
  134.3 3.9 %copy-start.16 = (bf16[2048,1,128]{2,0,1:T(8,128)(2,1)}, bf16[2048,1,128]{2,0,1:T(8,128)(2,1)S(1)}, u32[]{:S(2)}) copy-start(bf16[2048,1,128]{2,0,1:T(8,128)(2,1)S(1)} %get-tuple-element.410) | copy-start | bytes 1572868 | tf_op jit(solution)/shard_map/while
  139.1 4.1 %copy-start.1 = (f32[512,2048]{1,0:T(8,128)S(1)}, f32[512,2048]{1,0:T(8,128)}, u32[]{:S(2)}) copy-start(f32[512,2048]{1,0:T(8,128)} %copy-done) | copy-start | bytes 12582916 | tf_op jit(solution)/shard_map/while
  139.1 4.1 %copy-start.13 = (f32[2048,1,128]{0,2,1:T(8,128)S(1)}, f32[2048,1,128]{0,2,1:T(8,128)}, u32[]{:S(2)}) copy-start(f32[2048,1,128]{0,2,1:T(8,128)} %get-tuple-element.391) | copy-start | bytes 3145732 | tf_op jit(solution)/shard_map/while
  150.9 42.5 %copy-start.21 = (f32[128]{0:T(128)S(1)}, f32[128]{0:T(128)}, u32[]{:S(2)}) copy-start(f32[128]{0:T(128)} %param.14) | copy-start | bytes 1540
  151.8 15.4 %all-to-all-start.4 = ((bf16[16,2,8192]{2,1,0:T(2,128)(2,1)}), bf16[16,2,8192]{2,1,0:T(2,128)(2,1)S(1)}, u32[]{:S(2)}, u32[]{:S(2)}) async-start(bf16[16,2,8192]{2,1,0:T(2,128)(2,1)} %reshape.261), calls=%async_computation.4 | async-start | bytes 1048576 | tf_op jit(solution)/shard_map/all_to_all | solution.py:103
  188.8 21.9 %all-to-all-start.5 = ((f32[2048,1,128]{2,1,0:T(1,128)}), f32[2048,1,128]{2,1,0:T(1,128)S(1)}, u32[]{:S(2)}, u32[]{:S(2)}) async-start(f32[2048,1,128]{2,1,0:T(1,128)} %bitcast.206), calls=%async_computation.5 | async-start | bytes 2097152 | tf_op jit(solution)/shard_map/all_to_all | solution.py:106
  210.7 5.0 %copy-start.10 = (f32[2048,1,128]{2,1,0:T(1,128)}, f32[2048,1,128]{2,1,0:T(1,128)S(1)}, u32[]{:S(2)}) copy-start(f32[2048,1,128]{2,1,0:T(1,128)S(1)} %all-to-all-done.5) | copy-start | bytes 3145732
  210.7 22.4 %all-to-all-start.7 = ((f32[2048,1,128]{2,1,0:T(1,128)}), f32[2048,1,128]{2,1,0:T(1,128)}, u32[]{:S(2)}, u32[]{:S(2)}) async-start(f32[2048,1,128]{2,1,0:T(1,128)} %copy.116), calls=%async_computation.7 | async-start | bytes 2097152 | tf_op jit(solution)/shard_map/all_to_all | solution.py:108
  216.3 5.0 %copy-start.9 = (f32[128,8,128]{0,2,1:T(8,128)S(1)}, f32[128,8,128]{0,2,1:T(8,128)}, u32[]{:S(2)}) copy-start(f32[128,8,128]{0,2,1:T(8,128)} %copy-done.8) | copy-start | bytes 1572868
  217.6 7.3 %copy-start.5 = (f32[128,16,128]{0,2,1:T(8,128)S(1)}, f32[128,16,128]{0,2,1:T(8,128)}, u32[]{:S(2)}) copy-start(f32[128,16,128]{0,2,1:T(8,128)} %copy-done.4) | copy-start | bytes 3145732
  218.7 6.6 %copy-start.7 = (bf16[1,128,2048]{1,2,0:T(8,128)(2,1)S(1)}, bf16[1,128,2048]{1,2,0:T(8,128)(2,1)}, u32[]{:S(2)}) copy-start(bf16[1,128,2048]{1,2,0:T(8,128)(2,1)} %copy-done.6) | copy-start | bytes 1572868
  (28 other events, 69.6 us)
where the time goes:
time: 344 us; the launch traced here: 342 us
  blocking collectives  152 us (44%)
  waiting for transfers between devices  60.9 us (18%)
  matrix products  48 us (14%)
  starting transfers between devices  38.2 us (11%)
  local copies, waits for them, and re-layouts  28.6 us (8%)
  other arithmetic  12.9 us (4%)
    psum x1, blocking collectives, shards(): total_q, total_k = lax.psum((part_q, key_portion), ('dp', 'seq'))  106 us
    all_gather x1, blocking collectives, shards(): segment_all = lax.all_gather(segment_ids[0], 'seq', axis=0, tiled=True)  24.3 us
    all_to_all x1, blocking collectives, shards(): lax.all_to_all(key_gradient, 'seq', split_axis=0, concat_axis=1, tiled=True)  21.6 us
    all_to_all x1, waiting for transfers between devices, shards(): lax.all_to_all(grad_query, 'seq', split_axis=0, concat_axis=1, tiled=True)  13.7 us
    all_to_all x1, waiting for transfers between devices, shards(): lax.all_to_all(g_send, 'seq', split_axis=1, concat_axis=0, tiled=True)  11.3 us
    unnamed x39, local copies, waits for them, and re-layouts  10.8 us
    all_to_all x1, waiting for transfers between devices, shards(): lax.all_to_all(k_send, 'seq', split_axis=1, concat_axis=0, tiled=True)  10.4 us
    all_to_all x1, starting transfers between devices, shards(): lax.all_to_all(query_gain_scaled, 'seq', split_axis=1, concat_axis=0, til...  10.4 us
  transfers between devices with their start and end apart: 7, of which 6 were waited for; matrix products, arithmetic and copies ran while one was open for 5% of the time, Pallas kernels for 0%

commit v1 on v0

v1 whole, which is shorter than its diff:
```python
import functools
import math

import jax
import jax.numpy as jnp
from jax import lax
from jax.experimental import pallas as pl
from jax.experimental.pallas import tpu as pltpu
from jax.sharding import PartitionSpec as P

MESH = pl.DeviceIdType.MESH
EPSILON = 1e-06
D = 128
TOK = 128
SEQ = 16
HEADS_KV = 8
LEN = TOK * SEQ
B = 256
NB = LEN // B
BAND = 5
PAD = LEN + B
ONES = 16
FAR = -16384.0
F32, BF16 = jnp.float32, jnp.bfloat16
NT = (((1,), (1,)), ((), ()))


def _rows(start, count):
    return pl.ds(pl.multiple_of(start, count), count)


def _dot(a, b):
    return jnp.dot(a, b, preferred_element_type=F32)


def _inverse_norm(x):
    return lax.rsqrt(jnp.mean(x * x, axis=-1, keepdims=True) + EPSILON)


def _norm_backward(grad, inverse, unit, gain):
    scaled = grad * gain
    return inverse * (scaled - unit * jnp.mean(scaled * unit, axis=-1, keepdims=True))


def _fold(x):
    return jnp.sum(x.reshape(x.shape[0] // 8, 8, D), axis=0)


def _grouped(body):
    for first, last, blocks in ((0, 4, BAND), (4, 6, 4), (6, 8, 2)):
        lax.fori_loop(first, last, lambda j, _, blocks=blocks: (body(j, blocks), 0)[1], 0)


def kernel(
    q_in, k_in, v_in, g_in, seg_in, qg_in, kg_in,
    o_out, dq_out, dk_out, dv_out, gain_out,
    q_buf, k_buf, v_aug, g_aug, seg_buf, q_aug, k_aug, k_t, v_t, e_buf,
    o_acc, o32, o_bf, inv_col, inv_row, g_inv, q_inv, dq_acc, dk_buf, dv_buf, x_k, x_v,
    gq_bf, gk_bf, gv_bf, part, gain_src, gain_seq, z_src, z_four, zq_src, z_all,
    ss, rs, rs_k, rs_v, rs_xk, rs_xv,
):
    dp, me = lax.axis_index("dp"), lax.axis_index("seq")
    chip, core = me // 2, me % 2
    sib = me + 1 - 2 * core
    x_lo, z = dp // 16, dp % 16
    score_scale = D ** (-0.5)
    exponent_scale = score_scale * math.log2(math.e)

    (S_SEG, S_K, S_Q, S_V, S_G, S_KF, S_VF, S_O, S_DQ, S_XK, S_XV, S_DK, S_DV, S_GAIN, S_Z4, S_Z4B, S_ZA, S_Z5) = range(18)

    def at_seq(i):
        return (dp, i)

    def at_z(dx, dz):
        return (((x_lo + dx) % 2) * 16 + (z + dz + 16) % 16, me)

    z_peers = [at_z(0, 4), at_z(0, -4), at_z(0, 1), at_z(0, -1), at_z(0, 2), at_z(0, -2)]
    z_peers += [at_z(1, 0), at_z(1, 1), at_z(1, -1), at_z(1, 2), at_z(1, -2)]

    barrier = pltpu.get_barrier_semaphore()

    def greet(k, _):
        pl.semaphore_signal(barrier, inc=1, device_id=at_seq((me + k) % SEQ), device_id_type=MESH)
        return 0

    lax.fori_loop(1, SEQ, greet, 0)
    for peer in z_peers:
        pl.semaphore_signal(barrier, inc=1, device_id=peer, device_id_type=MESH)

    zero_block = jnp.zeros((B, D), F32)
    lane = lax.broadcasted_iota(jnp.int32, (D, D), 1)
    v_aug[:, D:] = jnp.ones((LEN, D), BF16)
    v_t[D:, :] = jnp.ones((ONES, LEN), BF16)
    o_acc[...] = jnp.zeros_like(o_acc)
    dq_acc[...] = jnp.zeros_like(dq_acc)
    part[...] = jnp.zeros_like(part)
    q_aug[LEN:, :D] = zero_block.astype(BF16)
    q_aug[LEN:, D:] = jnp.ones((B, D), BF16)
    g_aug[LEN:, :] = jnp.zeros((B, 2 * D), BF16)
    g_inv[LEN:, :] = zero_block.astype(BF16)
    q_inv[LEN:, :] = zero_block.astype(BF16)

    pl.semaphore_wait(barrier, SEQ - 1 + len(z_peers))

    def remote(src, dst, send, recv, peer):
        pltpu.make_async_remote_copy(src_ref=src, dst_ref=dst, send_sem=send, recv_sem=recv, device_id=peer, device_id_type=MESH).start()

    def local(src, dst, sem):
        pltpu.make_async_copy(src, dst, sem).start()

    def drain(ref, sem):
        pltpu.make_async_copy(ref, ref, sem).wait()

    mine = _rows(me * TOK, TOK)

    def send_seg(k, _):
        remote(seg_in, seg_buf.at[pl.ds(me, 1)], ss.at[S_SEG], rs.at[S_SEG], at_seq((me + k) % SEQ))
        return 0

    local(seg_in, seg_buf.at[pl.ds(me, 1)], rs.at[S_SEG])
    lax.fori_loop(1, SEQ, send_seg, 0)

    def send_heads(src, dst, s):
        local(src.at[0, :, _rows(me * D, D)], dst, rs.at[s])

        def one(k, _):
            to = (me + k) % SEQ
            remote(src.at[0, :, _rows(to * D, D)], dst, ss.at[s], rs.at[s], at_seq(to))
            return 0

        lax.fori_loop(1, SEQ, one, 0)

    def send_key_heads(src, dst, s, sems):
        local(src.at[0, :, _rows(chip * D, D)], dst, sems.at[chip])

        def one(k, _):
            to = (me + 2 * k) % SEQ
            remote(src.at[0, :, _rows((to // 2) * D, D)], dst, ss.at[s], sems.at[chip], at_seq(to))
            return 0

        lax.fori_loop(1, SEQ // 2, one, 0)

    send_key_heads(k_in, k_buf.at[mine], S_K, rs_k)
    send_heads(q_in, q_buf.at[mine], S_Q)
    send_key_heads(v_in, v_aug.at[mine, pl.ds(0, D)], S_V, rs_v)
    send_heads(g_in, g_aug.at[mine, pl.ds(0, D)], S_G)

    drain(seg_buf, rs.at[S_SEG])

    def documents(i, _):
        ids = seg_buf[pl.ds(i, 1), :].astype(F32)
        column = jnp.transpose(jnp.broadcast_to(ids, (D, D)))
        same = column == lane.astype(F32)
        rows = _rows(i * TOK, TOK)
        q_aug[rows, D:] = jnp.where(same, 1.0, 0.0).astype(BF16)
        k_aug[rows, D:] = jnp.where(same | (lane > 3), 0.0, FAR).astype(BF16)
        return 0

    lax.fori_loop(0, SEQ, documents, 0)

    def forward(k, sems, s, view):
        owner = (me - 2 * k + SEQ) % SEQ
        ref = view(_rows(owner * TOK, TOK))
        drain(ref, sems.at[owner // 2])
        remote(ref, ref, ss.at[s], rs.at[s], at_seq(sib))

    def forward_key(k, _):
        forward(k, rs_k, S_KF, lambda rows: k_buf.at[rows])
        return 0

    lax.fori_loop(0, SEQ // 2, forward_key, 0)
    half = pl.ds(0, LEN // 2)
    drain(k_buf.at[half], rs.at[S_KF])

    def norm_keys(i, _):
        rows = _rows(i * B, B)
        x = k_buf[rows, :].astype(F32)
        scaled = (x * _inverse_norm(x) * kg_in[...]).astype(BF16)
        k_aug[rows, :D] = scaled
        k_t[:, rows] = jnp.transpose(scaled)
        return 0

    lax.fori_loop(0, NB, norm_keys, 0)

    drain(q_buf, rs.at[S_Q])

    def norm_queries(i, _):
        rows = _rows(i * B, B)
        x = q_buf[rows, :].astype(F32)
        q_aug[rows, :D] = (x * _inverse_norm(x) * qg_in[...]).astype(BF16)
        return 0

    lax.fori_loop(0, NB, norm_queries, 0)

    causal = lax.broadcasted_iota(jnp.int32, (B, B), 0) <= lax.broadcasted_iota(jnp.int32, (B, B), 1)

    def scores(j, blocks):
        rows = _rows(j * B, B)
        k_block = k_aug[rows, :]
        for b in range(blocks):
            q_block = q_aug[_rows((j + b) * B, B), :]
            s = lax.dot_general(k_block, q_block, NT, preferred_element_type=F32)
            e = jnp.exp2(s * exponent_scale)
            if b == 0:
                e = jnp.where(causal, e, 0.0)
            e_buf[rows, b * B : (b + 1) * B] = e.astype(BF16)
        forward(j, rs_v, S_VF, lambda rows: v_aug.at[rows, pl.ds(0, D)])

    _grouped(scores)

    drain(v_aug.at[half, pl.ds(0, D)], rs.at[S_VF])

    def transpose_values(i, _):
        rows = _rows(i * B, B)
        v_t[:D, rows] = jnp.transpose(v_aug[rows, :D])
        return 0

    lax.fori_loop(0, NB, transpose_values, 0)

    def attend(j, blocks):
        rows = _rows(j * B, B)
        v_block = v_t[:, rows]
        for b in range(blocks):
            cols = _rows((j + b) * B, B)
            o_acc[:, cols] += _dot(v_block, e_buf[rows, b * B : (b + 1) * B])

    _grouped(attend)

    def return_tiles(t, i, src, out, s):
        cols = _rows(me * D, D)
        ours, other = 2 * i + core, 2 * i + 1 - core
        dst = out.at[0, :, cols]
        remote(src.at[_rows(other * TOK, TOK)], dst, ss.at[s], rs.at[s], at_seq(other))

        @pl.when(t == 0)
        def _():
            local(src.at[mine], dst, rs.at[s])

        @pl.when(t != 0)
        def _():
            remote(src.at[_rows(ours * TOK, TOK)], dst, ss.at[s], rs.at[s], at_seq(ours))

    def finish_attended(t, _):
        i = (chip + t) % NB
        cols = _rows(i * B, B)
        inverse = 1.0 / o_acc[D : D + 8, cols]
        inv_row[pl.ds(pl.multiple_of(i * 8, 8), 8), :] = inverse
        o = jnp.transpose((o_acc[:D, cols].reshape(D // 8, 8, B) * inverse[None]).reshape(D, B))
        o32[cols, :] = o
        o_bf[cols, :] = o.astype(BF16)
        return_tiles(t, i, o_bf, o_out, S_O)
        column = jnp.transpose(jnp.broadcast_to(inverse[None], (D // 8, 8, B)).reshape(D, B))
        inv_col[cols, :] = column
        q_inv[cols, :] = (q_aug[cols, :D].astype(F32) * (column * score_scale)).astype(BF16)
        return 0

    lax.fori_loop(0, NB, finish_attended, 0)

    drain(g_aug.at[pl.ds(0, LEN), pl.ds(0, D)], rs.at[S_G])
    lanes_b = lax.broadcasted_iota(jnp.int32, (B, D), 1)

    def row_terms(i, _):
        rows = _rows(i * B, B)
        g = g_aug[rows, :D].astype(F32)
        g_inv[rows, :] = (g * inv_col[rows, :]).astype(BF16)
        r = -jnp.sum(o32[rows, :] * g, axis=-1, keepdims=True)
        r1 = r.astype(BF16).astype(F32)
        r2 = (r - r1).astype(BF16).astype(F32)
        r3 = r - r1 - r2
        terms = jnp.where(lanes_b == 0, r1, jnp.where(lanes_b == 1, r2, jnp.where(lanes_b == 2, r3, 0.0)))
        g_aug[rows, D:] = terms.astype(BF16)
        return 0

    lax.fori_loop(0, NB, row_terms, 0)

    def backward(j, blocks):
        rows = _rows(j * B, B)
        v_block = v_aug[rows, :]
        k_block_t = k_t[:, rows]
        dk = dv = jnp.zeros((B, D), F32)
        for b in range(blocks):
            cols = _rows((j + b) * B, B)
            e = e_buf[rows, b * B : (b + 1) * B]
            gw = lax.dot_general(v_block, g_aug[cols, :], NT, preferred_element_type=F32)
            ds = (e.astype(F32) * gw).astype(BF16)
            dv = dv + _dot(e, g_inv[cols, :])
            dk = dk + _dot(ds, q_inv[cols, :])
            dq_acc[:, cols] += _dot(k_block_t, ds)
        dk_buf[rows, :] = dk
        dv_buf[rows, :] = dv

    def exchange(j):
        theirs = _rows((2 * j + 1 - core) * TOK, TOK)
        slot = _rows(j * TOK, TOK)
        remote(dk_buf.at[theirs], x_k.at[slot], ss.at[S_XK], rs_xk.at[j], at_seq(sib))
        remote(dv_buf.at[theirs], x_v.at[slot], ss.at[S_XV], rs_xv.at[j], at_seq(sib))

    def finish_keys(t):
        j = (chip + t) % NB
        owner = 2 * j + core
        ours, slot = _rows(owner * TOK, TOK), _rows(j * TOK, TOK)
        drain(x_k.at[slot], rs_xk.at[j])
        drain(x_v.at[slot], rs_xv.at[j])
        gv_bf[slot, :] = (dv_buf[ours, :] + x_v[slot, :]).astype(BF16)
        x = k_buf[ours, :].astype(F32)
        inverse = _inverse_norm(x)
        unit = x * inverse
        dk = dk_buf[ours, :] + x_k[slot, :]
        part[8:, :] += _fold(dk * unit)
        gk_bf[slot, :] = _norm_backward(dk, inverse, unit, kg_in[...]).astype(BF16)
        cols = _rows(chip * D, D)

        @pl.when(t == 0)
        def _():
            local(gk_bf.at[slot], dk_out.at[0, :, cols], rs.at[S_DK])
            local(gv_bf.at[slot], dv_out.at[0, :, cols], rs.at[S_DV])

        @pl.when(t != 0)
        def _():
            remote(gk_bf.at[slot], dk_out.at[0, :, cols], ss.at[S_DK], rs.at[S_DK], at_seq(owner))
            remote(gv_bf.at[slot], dv_out.at[0, :, cols], ss.at[S_DV], rs.at[S_DV], at_seq(owner))

    def backward_step(t, _):
        j = (chip + t) % NB
        for first, last, blocks in ((0, 4, BAND), (4, 6, 4), (6, 8, 2)):

            @pl.when((j >= first) & (j < last))
            def _(blocks=blocks):
                backward(j, blocks)

        exchange(j)

        @pl.when(t > 0)
        def _():
            finish_keys(t - 1)

        return 0

    lax.fori_loop(0, NB, backward_step, 0)

    def finish_queries(t, _):
        i = (chip + t) % NB
        rows = _rows(i * B, B)
        inverse_row = inv_row[pl.ds(pl.multiple_of(i * 8, 8), 8), :] * score_scale
        dq = jnp.transpose((dq_acc[:, rows].reshape(D // 8, 8, B) * inverse_row[None]).reshape(D, B))
        x = q_buf[rows, :].astype(F32)
        inverse = _inverse_norm(x)
        unit = x * inverse
        part[:8, :] += _fold(dq * unit)
        gq_bf[rows, :] = _norm_backward(dq, inverse, unit, qg_in[...]).astype(BF16)
        return_tiles(t, i, gq_bf, dq_out, S_DQ)
        return 0

    lax.fori_loop(0, NB, finish_queries, 0)
    finish_keys(NB - 1)

    totals = jnp.sum(part[...].reshape(2, 8, D), axis=1)
    gain_src[...] = jnp.concatenate([totals, jnp.zeros((6, D), F32)], axis=0)

    def send_gain(k, _):
        remote(gain_src, gain_seq.at[me], ss.at[S_GAIN], rs.at[S_GAIN], at_seq((me + k) % SEQ))
        return 0

    lax.fori_loop(1, SEQ, send_gain, 0)
    gain_seq[me] = gain_src[...]
    drain(gain_seq.at[pl.ds(0, SEQ - 1)], rs.at[S_GAIN])
    trajectory = jnp.sum(gain_seq[...], axis=0)
    z_src[...] = trajectory
    four = z // 4
    z_four[four] = trajectory
    remote(z_src, z_four.at[four], ss.at[S_Z4], rs.at[S_Z4], at_z(0, 4))
    remote(z_src, z_four.at[four], ss.at[S_Z4], rs.at[S_Z5], at_z(0, -4))
    ahead = z_four.at[(four + 1) % 4]
    drain(ahead, rs.at[S_Z5])
    remote(ahead, ahead, ss.at[S_Z4B], rs.at[S_Z4B], at_z(0, -4))
    drain(z_four.at[(four + 3) % 4], rs.at[S_Z4])
    drain(z_four.at[(four + 2) % 4], rs.at[S_Z4B])
    column_sum = z_four[0] + z_four[1] + z_four[2] + z_four[3]
    zq_src[...] = column_sum
    place = x_lo * 4 + z % 4
    z_all[place] = column_sum
    last_peers = [at_z(0, 1), at_z(0, -1), at_z(0, 2), at_z(1, 0), at_z(1, 1), at_z(1, -1), at_z(1, 2)]
    for peer in last_peers:
        remote(zq_src, z_all.at[place], ss.at[S_ZA], rs.at[S_ZA], peer)
    drain(z_all.at[pl.ds(0, 7)], rs.at[S_ZA])
    gain_out[...] = jnp.sum(z_all[...], axis=0)

    drain(o_out.at[0], rs.at[S_O])
    drain(dq_out.at[0], rs.at[S_DQ])
    drain(dk_out.at[0], rs.at[S_DK])
    drain(dv_out.at[0], rs.at[S_DV])
    most, some = pl.ds(0, LEN - TOK), pl.ds(0, LEN // 2 - TOK)
    drain(seg_buf.at[pl.ds(0, SEQ - 1)], ss.at[S_SEG])
    drain(k_buf.at[some], ss.at[S_K])
    drain(q_buf.at[most], ss.at[S_Q])
    drain(k_buf.at[some], ss.at[S_V])
    drain(q_buf.at[most], ss.at[S_G])
    drain(k_buf.at[half], ss.at[S_KF])
    drain(k_buf.at[half], ss.at[S_VF])
    drain(o_bf.at[most], ss.at[S_O])
    drain(gq_bf.at[most], ss.at[S_DQ])
    drain(x_k, ss.at[S_XK])
    drain(x_v, ss.at[S_XV])
    drain(gk_bf.at[some], ss.at[S_DK])
    drain(gv_bf.at[some], ss.at[S_DV])
    drain(gain_seq.at[pl.ds(0, SEQ - 1)], ss.at[S_GAIN])
    drain(z_four.at[pl.ds(0, 2)], ss.at[S_Z4])
    drain(z_four.at[0], ss.at[S_Z4B])
    drain(z_all.at[pl.ds(0, 7)], ss.at[S_ZA])


def shards(q_raw, key_unnormed, value_input, grad_attended, segment_ids, q_gain, key_norm_gain):
    hbm = pl.BlockSpec(memory_space=pl.ANY)
    vmem = pl.BlockSpec(memory_space=pltpu.VMEM)
    q_heads, kv_heads = q_raw.shape[2] // D, key_unnormed.shape[2] // D
    dma = pltpu.SemaphoreType.DMA
    out = pl.pallas_call(
        kernel,
        out_shape=[
            jax.ShapeDtypeStruct(q_raw.shape, BF16),
            jax.ShapeDtypeStruct(q_raw.shape, BF16),
            jax.ShapeDtypeStruct(key_unnormed.shape, BF16),
            jax.ShapeDtypeStruct(key_unnormed.shape, BF16),
            jax.ShapeDtypeStruct((8, D), F32),
        ],
        in_specs=[hbm] * 5 + [vmem] * 2,
        out_specs=[hbm] * 4 + [vmem],
        scratch_shapes=[
            pltpu.VMEM((LEN, D), BF16),
            pltpu.VMEM((LEN, D), BF16),
            pltpu.VMEM((LEN, 2 * D), BF16),
            pltpu.VMEM((PAD, 2 * D), BF16),
            pltpu.VMEM((SEQ, TOK), jnp.int32),
            pltpu.VMEM((PAD, 2 * D), BF16),
            pltpu.VMEM((LEN, 2 * D), BF16),
            pltpu.VMEM((D, LEN), BF16),
            pltpu.VMEM((D + ONES, LEN), BF16),
            pltpu.VMEM((LEN, BAND * B), BF16),
            pltpu.VMEM((D + ONES, PAD), F32),
            pltpu.VMEM((LEN, D), F32),
            pltpu.VMEM((LEN, D), BF16),
            pltpu.VMEM((LEN, D), F32),
            pltpu.VMEM((NB * 8, B), F32),
            pltpu.VMEM((PAD, D), BF16),
            pltpu.VMEM((PAD, D), BF16),
            pltpu.VMEM((D, PAD), F32),
            pltpu.VMEM((LEN, D), F32),
            pltpu.VMEM((LEN, D), F32),
            pltpu.VMEM((LEN // 2, D), F32),
            pltpu.VMEM((LEN // 2, D), F32),
            pltpu.VMEM((LEN, D), BF16),
            pltpu.VMEM((LEN // 2, D), BF16),
            pltpu.VMEM((LEN // 2, D), BF16),
            pltpu.VMEM((16, D), F32),
            pltpu.VMEM((8, D), F32),
            pltpu.VMEM((SEQ, 8, D), F32),
            pltpu.VMEM((8, D), F32),
            pltpu.VMEM((4, 8, D), F32),
            pltpu.VMEM((8, D), F32),
            pltpu.VMEM((8, 8, D), F32),
            dma((18,)),
            dma((18,)),
            dma((8,)),
            dma((8,)),
            dma((8,)),
            dma((8,)),
        ],
        compiler_params=pltpu.CompilerParams(
            collective_id=0, has_side_effects=True, vmem_limit_bytes=52 << 20
        ),
        name="attention",
    )(
        q_raw,
        key_unnormed,
        value_input,
        grad_attended,
        segment_ids,
        q_gain.reshape(1, D),
        key_norm_gain.reshape(1, D),
    )
    attended, grad_q, grad_k, grad_value, gains = out
    tokens = lax.axis_size("dp") * lax.axis_size("seq") * q_raw.shape[1]
    grad_q_gain = gains[0] / math.sqrt(tokens * q_heads)
    key_gain_gradient = gains[1] / math.sqrt(tokens * kv_heads)
    return attended, grad_q, grad_k, grad_value, grad_q_gain, key_gain_gradient


def solution(mesh):
    tokens = P("dp", "seq", None)
    in_specs = (tokens, tokens, tokens, tokens, P("dp", "seq"), P(), P())
    out_specs = (tokens, tokens, tokens, tokens, P(), P())
    return jax.shard_map(shards, mesh=mesh, in_specs=in_specs, out_specs=out_specs, check_vma=False)
```

time: 344 us -> 83.5 us (0.24)
  the two profiles are of different devices: /device:TPU:1 before, /device:TPU:12 now
where the time goes in v1:
time: 83.5 us; the launch traced here: 83.2 us
  Pallas kernels  76 us (91%)
  local copies, waits for them, and re-layouts  5.99 us (7%)
    pallas_call x1, Pallas kernels, shards(): pl.pallas_call(kernel, out_shape=[jax.ShapeDtypeStruct(q_raw.shape, BF16)...  76 us
    unnamed x16, local copies, waits for them, and re-layouts  5.99 us

profile of v1, /device:TPU:12, one launch (start us, length us, event | category | flops | bytes accessed | tf_op | source)
XLA Modules:
  0.0 83.2 jit_solution(18425047417837329184)
XLA Ops:
  0.6 0.0 copy-start.2
  0.6 0.0 copy-start.3
  0.7 0.0 copy-start.4
  0.7 0.6 copy-done.2
  1.3 0.0 copy-done.3
  1.3 0.0 copy-done.4
  1.3 0.0 copy-start
  1.3 0.9 %copy-done = bf16[1,128,1024]{2,1,0:T(8,128)(2,1)S(1)} copy-done((bf16[1,128,1024]{2,1,0:T(8,128)(2,1)S(1)}, bf16[1,128,1024]{2,1,0:T(8,128)(2,1)}, u32[]{:S(2)}) %copy-start) | copy-done | bytes 262168
  2.3 0.0 copy-start.1
  2.3 0.9 %copy-done.1 = bf16[1,128,1024]{2,1,0:T(8,128)(2,1)S(1)} copy-done((bf16[1,128,1024]{2,1,0:T(8,128)(2,1)S(1)}, bf16[1,128,1024]{2,1,0:T(8,128)(2,1)}, u32[]{:S(2)}) %copy-start.1) | copy-done | bytes 262168
  3.2 76.0 %attention.1 = (bf16[1,128,2048]{2,1,0:T(8,128)(2,1)S(1)}, bf16[1,128,2048]{2,1,0:T(8,128)(2,1)}, bf16[1,128,1024]{2,1,0:T(8,128)(2,1)S(1)}, bf16[1,128,1024]{2,1,0:T(8,128)(2,1)S(1)}, f32[8,128]{1,0:T(8,128)S(1)}) custom-call(bf16[1,128,2048]{2,1,0:T(8,128)(2,1)} %q_in.1, bf16[1,128,1024]{2,1,0:T(8,128)(2,1)S(1)} %copy-done, ...), custom_call_target="tpu_custom_call" | custom-call | tf_op jit(solution)/shard_map/attention/pallas_call | solution.py:417
  79.3 0.5 multiply_bitcast_fusion
  79.8 0.0 copy-start.5
  79.8 0.8 copy.17
  80.6 0.4 copy-done.5
  81.0 0.8 copy.18
  81.8 0.7 copy.19
  82.5 0.7 copy.20
Async XLA Ops:
  0.6 0.7 copy-start.2
  0.6 0.7 copy-start.3
  0.7 0.7 copy-start.4
  1.3 0.9 %copy-start = (bf16[1,128,1024]{2,1,0:T(8,128)(2,1)S(1)}, bf16[1,128,1024]{2,1,0:T(8,128)(2,1)}, u32[]{:S(2)}) copy-start(bf16[1,128,1024]{2,1,0:T(8,128)(2,1)} %k_in.1) | copy-start | bytes 786436
  2.3 0.9 %copy-start.1 = (bf16[1,128,1024]{2,1,0:T(8,128)(2,1)S(1)}, bf16[1,128,1024]{2,1,0:T(8,128)(2,1)}, u32[]{:S(2)}) copy-start(bf16[1,128,1024]{2,1,0:T(8,128)(2,1)} %v_in.1) | copy-start | bytes 786436
  79.8 1.2 %copy-start.5 = (bf16[1,128,2048]{2,1,0:T(8,128)(2,1)S(1)}, bf16[1,128,2048]{2,1,0:T(8,128)(2,1)}, u32[]{:S(2)}) copy-start(bf16[1,128,2048]{2,1,0:T(8,128)(2,1)} %get-tuple-element.25) | copy-start | bytes 1572868

commit v2 on v1

v2 whole, which is shorter than its diff:
```python
import functools
import math

import jax
import jax.numpy as jnp
from jax import lax
from jax.experimental import pallas as pl
from jax.experimental.pallas import tpu as pltpu
from jax.sharding import PartitionSpec as P

MESH = pl.DeviceIdType.MESH
EPSILON = 1e-06
D = 128
TOK = 128
SEQ = 16
HEADS_KV = 8
LEN = TOK * SEQ
B = 256
NB = LEN // B
STEPS = 2
BAND = 5
ONES = 16
FAR = -16384.0
F32, BF16 = jnp.float32, jnp.bfloat16
NT = (((1,), (1,)), ((), ()))


def _rows(start, count):
    return pl.ds(pl.multiple_of(start, count), count)


def _dot(a, b):
    return jnp.dot(a, b, preferred_element_type=F32)


def _inverse_norm(x):
    return lax.rsqrt(jnp.mean(x * x, axis=-1, keepdims=True) + EPSILON)


def _norm_backward(grad, inverse, unit, gain):
    scaled = grad * gain
    return inverse * (scaled - unit * jnp.mean(scaled * unit, axis=-1, keepdims=True))


def _fold(x):
    return jnp.sum(x.reshape(x.shape[0] // 8, 8, D), axis=0)


def _blocks(j):
    return range(j, min(j + BAND, NB))


def _first_key(i):
    return max(0, i - BAND + 1)


def kernel(
    q_in, k_in, v_in, g_in, seg_in, qg_in, kg_in,
    o_out, dq_out, dk_out, dv_out, gain_out,
    q_buf, k_buf, v_aug, g_aug, seg_buf, q_aug, k_aug, k_t, v_t, e_keys, e_queries, ds_keys, q_unit, q_norm,
    o32, o_bf, inv_col, inv_row, g_inv, q_inv, dq_acc, dk_buf, dv_buf, x_k, x_v,
    gq_bf, gk_bf, gv_bf, qg, kg, part, gain_seq, z_src, z_four, zq_src, z_all,
    ss, rs, rs_k, rs_v, rs_xk, rs_xv,
):
    dp, me = lax.axis_index("dp"), lax.axis_index("seq")
    chip, core = me // 2, me % 2
    sib = me + 1 - 2 * core
    x_lo, z = dp // 16, dp % 16
    score_scale = D ** (-0.5)
    exponent_scale = score_scale * math.log2(math.e)

    (S_SEG, S_K, S_Q, S_V, S_G, S_KF, S_VF, S_O, S_DQ, S_XK, S_XV, S_DK, S_DV, S_GAIN, S_Z4, S_Z4B, S_ZA, S_Z5, S_QG, S_KG) = range(20)

    def at_seq(i):
        return (dp, i)

    def at_z(dx, dz):
        return (((x_lo + dx) % 2) * 16 + (z + dz + 16) % 16, me)

    z_peers = [at_z(0, 4), at_z(0, -4), at_z(0, 1), at_z(0, -1), at_z(0, 2), at_z(0, -2)]
    z_peers += [at_z(1, 0), at_z(1, 1), at_z(1, -1), at_z(1, 2), at_z(1, -2)]

    barrier = pltpu.get_barrier_semaphore()

    def greet(k, _):
        pl.semaphore_signal(barrier, inc=1, device_id=at_seq((me + k) % SEQ), device_id_type=MESH)
        return 0

    lax.fori_loop(1, SEQ, greet, 0)
    for peer in z_peers:
        pl.semaphore_signal(barrier, inc=1, device_id=peer, device_id_type=MESH)

    lane = lax.broadcasted_iota(jnp.int32, (D, D), 1)
    v_aug[:, D:] = jnp.ones((LEN, D), BF16)
    v_t[D:, :] = jnp.ones((ONES, LEN), BF16)
    pltpu.make_async_copy(qg_in, qg, rs.at[S_QG]).start()
    pltpu.make_async_copy(kg_in, kg, rs.at[S_KG]).start()

    pl.semaphore_wait(barrier, SEQ - 1 + len(z_peers))

    def remote(src, dst, send, recv, peer):
        pltpu.make_async_remote_copy(src_ref=src, dst_ref=dst, send_sem=send, recv_sem=recv, device_id=peer, device_id_type=MESH).start()

    def local(src, dst, sem):
        pltpu.make_async_copy(src, dst, sem).start()

    def drain(ref, sem):
        pltpu.make_async_copy(ref, ref, sem).wait()

    mine = _rows(me * TOK, TOK)

    def send_seg(k, _):
        remote(seg_in, seg_buf.at[pl.ds(me, 1)], ss.at[S_SEG], rs.at[S_SEG], at_seq((me + k) % SEQ))
        return 0

    local(seg_in, seg_buf.at[pl.ds(me, 1)], rs.at[S_SEG])
    lax.fori_loop(1, SEQ, send_seg, 0)

    def send_heads(src, dst, s):
        local(src.at[0, :, _rows(me * D, D)], dst, rs.at[s])

        def one(k, _):
            to = (me + k) % SEQ
            remote(src.at[0, :, _rows(to * D, D)], dst, ss.at[s], rs.at[s], at_seq(to))
            return 0

        lax.fori_loop(1, SEQ, one, 0)

    def send_key_heads(src, dst, s, sems):
        local(src.at[0, :, _rows(chip * D, D)], dst, sems.at[chip])

        def one(k, _):
            to = (me + 2 * k) % SEQ
            remote(src.at[0, :, _rows((to // 2) * D, D)], dst, ss.at[s], sems.at[chip], at_seq(to))
            return 0

        lax.fori_loop(1, SEQ // 2, one, 0)

    send_key_heads(k_in, k_buf.at[mine], S_K, rs_k)
    send_key_heads(v_in, v_aug.at[mine, pl.ds(0, D)], S_V, rs_v)
    send_heads(q_in, q_buf.at[mine], S_Q)
    send_heads(g_in, g_aug.at[mine, pl.ds(0, D)], S_G)

    drain(qg, rs.at[S_QG])
    drain(kg, rs.at[S_KG])
    drain(seg_buf, rs.at[S_SEG])

    def documents(i, _):
        ids = seg_buf[pl.ds(i, 1), :].astype(F32)
        column = jnp.transpose(jnp.broadcast_to(ids, (D, D)))
        same = column == lane.astype(F32)
        rows = _rows(i * TOK, TOK)
        q_aug[rows, D:] = jnp.where(same, 1.0, 0.0).astype(BF16)
        k_aug[rows, D:] = jnp.where(same | (lane > 3), 0.0, FAR).astype(BF16)
        return 0

    lax.fori_loop(0, SEQ, documents, 0, unroll=4)

    def forward(k, sems, s, view):
        owner = (me - 2 * k + SEQ) % SEQ
        ref = view(_rows(owner * TOK, TOK))
        drain(ref, sems.at[owner // 2])
        remote(ref, ref, ss.at[s], rs.at[s], at_seq(sib))

    def forward_key(k, _):
        forward(k, rs_k, S_KF, lambda rows: k_buf.at[rows])
        return 0

    lax.fori_loop(0, SEQ // 2, forward_key, 0)
    half = pl.ds(0, LEN // 2)
    drain(k_buf.at[half], rs.at[S_KF])

    def norm_keys(i, _):
        rows = _rows(i * B, B)
        x = k_buf[rows, :].astype(F32)
        scaled = (x * _inverse_norm(x) * kg[...]).astype(BF16)
        k_aug[rows, :D] = scaled
        k_t[:, rows] = jnp.transpose(scaled)
        return 0

    lax.fori_loop(0, NB, norm_keys, 0, unroll=4)

    def forward_value(k, _):
        forward(k, rs_v, S_VF, lambda rows: v_aug.at[rows, pl.ds(0, D)])
        return 0

    lax.fori_loop(0, SEQ // 2, forward_value, 0)
    drain(v_aug.at[half, pl.ds(0, D)], rs.at[S_VF])

    def transpose_values(i, _):
        rows = _rows(i * B, B)
        v_t[:D, rows] = jnp.transpose(v_aug[rows, :D])
        return 0

    lax.fori_loop(0, NB, transpose_values, 0, unroll=4)

    drain(q_buf, rs.at[S_Q])

    def norm_queries(i, _):
        rows = _rows(i * B, B)
        x = q_buf[rows, :].astype(F32)
        inverse = _inverse_norm(x)
        unit = x * inverse
        q_norm[rows, :] = jnp.broadcast_to(inverse, (B, D))
        q_unit[rows, :] = unit
        q_aug[rows, :D] = (unit * qg[...]).astype(BF16)
        return 0

    lax.fori_loop(0, NB, norm_queries, 0, unroll=4)
    causal = lax.broadcasted_iota(jnp.int32, (B, B), 0) <= lax.broadcasted_iota(jnp.int32, (B, B), 1)

    for j in range(NB):
        k_block = k_aug[j * B : (j + 1) * B, :]
        for i in _blocks(j):
            s = lax.dot_general(k_block, q_aug[i * B : (i + 1) * B, :], NT, preferred_element_type=F32)
            e = jnp.exp2(s * exponent_scale)
            if i == j:
                e = jnp.where(causal, e, 0.0)
            e = e.astype(BF16)
            e_keys[j * B : (j + 1) * B, (i - j) * B : (i - j + 1) * B] = e
            at = (i * BAND + j - _first_key(i)) * B
            e_queries[at : at + B, :] = e

    for i in range(NB):
        first, rows = _first_key(i), slice(i * B, (i + 1) * B)
        keys = (i + 1 - first) * B
        o_t = _dot(v_t[:, first * B : (i + 1) * B], e_queries[i * BAND * B : i * BAND * B + keys, :])
        inverse = 1.0 / o_t[D : D + 8, :]
        inv_row[i * 8 : (i + 1) * 8, :] = inverse
        o = jnp.transpose((o_t[:D, :].reshape(D // 8, 8, B) * inverse[None]).reshape(D, B))
        o32[rows, :] = o
        o_bf[rows, :] = o.astype(BF16)
        column = jnp.transpose(jnp.broadcast_to(inverse[None], (D // 8, 8, B)).reshape(D, B))
        inv_col[rows, :] = column
        q_inv[rows, :] = (q_aug[rows, :D].astype(F32) * (column * score_scale)).astype(BF16)

    def return_tiles(src, out, s):
        dst = out.at[0, :, _rows(me * D, D)]
        local(src.at[mine], dst, rs.at[s])
        remote(src.at[_rows(sib * TOK, TOK)], dst, ss.at[s], rs.at[s], at_seq(sib))

        def one(t, _):
            i = (chip + t) % NB
            ours, other = 2 * i + core, 2 * i + 1 - core
            remote(src.at[_rows(ours * TOK, TOK)], dst, ss.at[s], rs.at[s], at_seq(ours))
            remote(src.at[_rows(other * TOK, TOK)], dst, ss.at[s], rs.at[s], at_seq(other))
            return 0

        lax.fori_loop(1, NB, one, 0)

    return_tiles(o_bf, o_out, S_O)

    drain(g_aug.at[:, pl.ds(0, D)], rs.at[S_G])
    lanes_b = lax.broadcasted_iota(jnp.int32, (B, D), 1)

    for i in range(NB):
        rows = slice(i * B, (i + 1) * B)
        g = g_aug[rows, :D].astype(F32)
        g_inv[rows, :] = (g * inv_col[rows, :]).astype(BF16)
        r = -jnp.sum(o32[rows, :] * g, axis=-1, keepdims=True)
        r1 = r.astype(BF16).astype(F32)
        r2 = (r - r1).astype(BF16).astype(F32)
        r3 = r - r1 - r2
        terms = jnp.where(lanes_b == 0, r1, jnp.where(lanes_b == 1, r2, jnp.where(lanes_b == 2, r3, 0.0)))
        g_aug[rows, D:] = terms.astype(BF16)

    gain_part = jnp.zeros((8, D), F32)
    for j in range(NB):
        rows, queries = slice(j * B, (j + 1) * B), slice(j * B, (_blocks(j)[-1] + 1) * B)
        span = len(_blocks(j)) * B
        v_block = v_aug[rows, :]
        for i in _blocks(j):
            cols = slice((i - j) * B, (i - j + 1) * B)
            gw = lax.dot_general(v_block, g_aug[i * B : (i + 1) * B, :], NT, preferred_element_type=F32)
            ds_keys[j % 2, :, cols] = (e_keys[rows, cols].astype(F32) * gw).astype(BF16)
        ds = ds_keys[j % 2, :, :span]
        dv_buf[rows, :] = _dot(e_keys[rows, :span], g_inv[queries, :])
        dk = _dot(ds, q_inv[queries, :])
        dk_buf[rows, :] = dk
        gain_part = gain_part + _fold(dk * k_aug[rows, :D].astype(F32))
        part_dq = _dot(k_t[:, rows], ds)
        if j == 0:
            dq_acc[:, queries] = part_dq
        else:
            old = slice(queries.start, min(queries.stop, (j + BAND - 1) * B))
            width = old.stop - old.start
            dq_acc[:, old] += part_dq[:, :width]
            if width < span:
                dq_acc[:, old.stop : queries.stop] = part_dq[:, width:]
        theirs = _rows((2 * j + 1 - core) * TOK, TOK)
        slot = pl.ds(j * TOK, TOK)
        remote(dk_buf.at[theirs], x_k.at[slot], ss.at[S_XK], rs_xk.at[j], at_seq(sib))
        remote(dv_buf.at[theirs], x_v.at[slot], ss.at[S_XV], rs_xv.at[j], at_seq(sib))
    part[...] = gain_part

    def send_gain(k, _):
        remote(part, gain_seq.at[me], ss.at[S_GAIN], rs.at[S_GAIN], at_seq((me + k) % SEQ))
        return 0

    lax.fori_loop(1, SEQ, send_gain, 0)
    gain_seq[me] = part[...]

    for i in range(NB):
        rows = slice(i * B, (i + 1) * B)
        inverse_row = inv_row[i * 8 : (i + 1) * 8, :] * score_scale
        dq = jnp.transpose((dq_acc[:, rows].reshape(D // 8, 8, B) * inverse_row[None]).reshape(D, B))
        gq_bf[rows, :] = _norm_backward(dq, q_norm[rows, :], q_unit[rows, :], qg[...]).astype(BF16)
    return_tiles(gq_bf, dq_out, S_DQ)

    for j in range(NB):
        ours, slot = _rows((2 * j + core) * TOK, TOK), pl.ds(j * TOK, TOK)
        drain(x_k.at[slot], rs_xk.at[j])
        drain(x_v.at[slot], rs_xv.at[j])
        gv_bf[slot, :] = (dv_buf[ours, :] + x_v[slot, :]).astype(BF16)
        x = k_buf[ours, :].astype(F32)
        inverse = _inverse_norm(x)
        gk_bf[slot, :] = _norm_backward(dk_buf[ours, :] + x_k[slot, :], inverse, x * inverse, kg[...]).astype(BF16)

    key_cols = _rows(chip * D, D)
    dk_dst, dv_dst = dk_out.at[0, :, key_cols], dv_out.at[0, :, key_cols]
    local(gk_bf.at[_rows(chip * TOK, TOK)], dk_dst, rs.at[S_DK])
    local(gv_bf.at[_rows(chip * TOK, TOK)], dv_dst, rs.at[S_DV])

    def return_keys(t, _):
        j = (chip + t) % NB
        slot = _rows(j * TOK, TOK)
        remote(gk_bf.at[slot], dk_dst, ss.at[S_DK], rs.at[S_DK], at_seq(2 * j + core))
        remote(gv_bf.at[slot], dv_dst, ss.at[S_DV], rs.at[S_DV], at_seq(2 * j + core))
        return 0

    lax.fori_loop(1, NB, return_keys, 0)

    drain(gain_seq.at[pl.ds(0, SEQ - 1)], rs.at[S_GAIN])
    trajectory = jnp.sum(gain_seq[...], axis=0)
    z_src[...] = trajectory
    four = z // 4
    z_four[four] = trajectory
    remote(z_src, z_four.at[four], ss.at[S_Z4], rs.at[S_Z4], at_z(0, 4))
    remote(z_src, z_four.at[four], ss.at[S_Z4], rs.at[S_Z5], at_z(0, -4))
    ahead = z_four.at[(four + 1) % 4]
    drain(ahead, rs.at[S_Z5])
    remote(ahead, ahead, ss.at[S_Z4B], rs.at[S_Z4B], at_z(0, -4))
    drain(z_four.at[(four + 3) % 4], rs.at[S_Z4])
    drain(z_four.at[(four + 2) % 4], rs.at[S_Z4B])
    column_sum = z_four[0] + z_four[1] + z_four[2] + z_four[3]
    zq_src[...] = column_sum
    place = x_lo * 4 + z % 4
    z_all[place] = column_sum
    last_peers = [at_z(0, 1), at_z(0, -1), at_z(0, 2), at_z(1, 0), at_z(1, 1), at_z(1, -1), at_z(1, 2)]
    for peer in last_peers:
        remote(zq_src, z_all.at[place], ss.at[S_ZA], rs.at[S_ZA], peer)
    drain(z_all.at[pl.ds(0, 7)], rs.at[S_ZA])
    total = jnp.sum(jnp.sum(z_all[...], axis=0), axis=0, keepdims=True)
    gain_out[0:1, :] = total / qg[...]
    gain_out[1:2, :] = total / kg[...]

    drain(o_out.at[0], rs.at[S_O])
    drain(dq_out.at[0], rs.at[S_DQ])
    drain(dk_out.at[0], rs.at[S_DK])
    drain(dv_out.at[0], rs.at[S_DV])
    most, some = pl.ds(0, LEN - TOK), pl.ds(0, LEN // 2 - TOK)
    drain(seg_buf.at[pl.ds(0, SEQ - 1)], ss.at[S_SEG])
    drain(k_buf.at[some], ss.at[S_K])
    drain(q_buf.at[most], ss.at[S_Q])
    drain(k_buf.at[some], ss.at[S_V])
    drain(q_buf.at[most], ss.at[S_G])
    drain(k_buf.at[half], ss.at[S_KF])
    drain(k_buf.at[half], ss.at[S_VF])
    drain(o_bf.at[most], ss.at[S_O])
    drain(gq_bf.at[most], ss.at[S_DQ])
    drain(x_k, ss.at[S_XK])
    drain(x_v, ss.at[S_XV])
    drain(gk_bf.at[some], ss.at[S_DK])
    drain(gv_bf.at[some], ss.at[S_DV])
    drain(gain_seq.at[pl.ds(0, SEQ - 1)], ss.at[S_GAIN])
    drain(z_four.at[pl.ds(0, 2)], ss.at[S_Z4])
    drain(z_four.at[0], ss.at[S_Z4B])
    drain(z_all.at[pl.ds(0, 7)], ss.at[S_ZA])


def finish(o_in, dq_in, dk_in, dv_in, gains, o_out, dq_out, dk_out, dv_out, q_out, k_out, *, q_scale, k_scale):
    for src, dst in ((o_in, o_out), (dq_in, dq_out), (dk_in, dk_out), (dv_in, dv_out)):
        dst[...] = src[...]
    q_out[...] = gains[0:1, :] * q_scale
    k_out[...] = gains[1:2, :] * k_scale


def shards(q_raw, key_unnormed, value_input, grad_attended, segment_ids, q_gain, key_norm_gain):
    hbm = pl.BlockSpec(memory_space=pltpu.HBM)
    anywhere = pl.BlockSpec(memory_space=pl.ANY)
    vmem = pl.BlockSpec(memory_space=pltpu.VMEM)
    q_heads, kv_heads = q_raw.shape[2] // D, key_unnormed.shape[2] // D
    dma = pltpu.SemaphoreType.DMA
    results = [
        jax.ShapeDtypeStruct(q_raw.shape, BF16),
        jax.ShapeDtypeStruct(q_raw.shape, BF16),
        jax.ShapeDtypeStruct(key_unnormed.shape, BF16),
        jax.ShapeDtypeStruct(key_unnormed.shape, BF16),
    ]
    staged = pl.pallas_call(
        kernel,
        out_shape=results + [jax.ShapeDtypeStruct((8, D), F32)],
        in_specs=[hbm] * 7,
        out_specs=[anywhere] * 4 + [vmem],
        scratch_shapes=[
            pltpu.VMEM((LEN, D), BF16),
            pltpu.VMEM((LEN, D), BF16),
            pltpu.VMEM((LEN, 2 * D), BF16),
            pltpu.VMEM((LEN, 2 * D), BF16),
            pltpu.VMEM((SEQ, TOK), jnp.int32),
            pltpu.VMEM((LEN, 2 * D), BF16),
            pltpu.VMEM((LEN, 2 * D), BF16),
            pltpu.VMEM((D, LEN), BF16),
            pltpu.VMEM((D + ONES, LEN), BF16),
            pltpu.VMEM((LEN, BAND * B), BF16),
            pltpu.VMEM((NB * BAND * B, B), BF16),
            pltpu.VMEM((2, B, BAND * B), BF16),
            pltpu.VMEM((LEN, D), F32),
            pltpu.VMEM((LEN, D), F32),
            pltpu.VMEM((LEN, D), F32),
            pltpu.VMEM((LEN, D), BF16),
            pltpu.VMEM((LEN, D), F32),
            pltpu.VMEM((NB * 8, B), F32),
            pltpu.VMEM((LEN, D), BF16),
            pltpu.VMEM((LEN, D), BF16),
            pltpu.VMEM((D, LEN), F32),
            pltpu.VMEM((LEN, D), F32),
            pltpu.VMEM((LEN, D), F32),
            pltpu.VMEM((LEN // 2, D), F32),
            pltpu.VMEM((LEN // 2, D), F32),
            pltpu.VMEM((LEN, D), BF16),
            pltpu.VMEM((LEN // 2, D), BF16),
            pltpu.VMEM((LEN // 2, D), BF16),
            pltpu.VMEM((1, D), F32),
            pltpu.VMEM((1, D), F32),
            pltpu.VMEM((8, D), F32),
            pltpu.VMEM((SEQ, 8, D), F32),
            pltpu.VMEM((8, D), F32),
            pltpu.VMEM((4, 8, D), F32),
            pltpu.VMEM((8, D), F32),
            pltpu.VMEM((8, 8, D), F32),
            dma((20,)),
            dma((20,)),
            dma((8,)),
            dma((8,)),
            dma((8,)),
            dma((8,)),
        ],
        compiler_params=pltpu.CompilerParams(
            collective_id=0, has_side_effects=True, vmem_limit_bytes=60 << 20
        ),
        name="attention",
    )(
        q_raw,
        key_unnormed,
        value_input,
        grad_attended,
        segment_ids,
        q_gain.reshape(1, D),
        key_norm_gain.reshape(1, D),
    )
    tokens = lax.axis_size("dp") * lax.axis_size("seq") * q_raw.shape[1]
    row = jax.ShapeDtypeStruct((1, D), F32)
    tiles = [pl.BlockSpec((1, TOK // STEPS, r.shape[2]), lambda t: (0, t, 0)) for r in results]
    rows = [pl.BlockSpec((count, D), lambda t: (0, 0)) for count in (8, 1, 1)]
    *tiles, grad_q_gain, key_gain_gradient = pl.pallas_call(
        functools.partial(finish, q_scale=(tokens * q_heads) ** -0.5, k_scale=(tokens * kv_heads) ** -0.5),
        out_shape=results + [row, row],
        grid=(STEPS,),
        in_specs=tiles + rows[:1],
        out_specs=tiles + rows[1:],
        name="finish",
    )(*staged)
    return *tiles, grad_q_gain.reshape(D), key_gain_gradient.reshape(D)


def solution(mesh):
    tokens = P("dp", "seq", None)
    in_specs = (tokens, tokens, tokens, tokens, P("dp", "seq"), P(), P())
    out_specs = (tokens, tokens, tokens, tokens, P(), P())
    return jax.shard_map(shards, mesh=mesh, in_specs=in_specs, out_specs=out_specs, check_vma=False)
```

time: 83.5 us -> 64.8 us (0.78)
  the two profiles are of different devices: /device:TPU:12 before, /device:TPU:1 now
where the time goes in v2:
time: 64.8 us; the launch traced here: 64.3 us
  Pallas kernels  63.7 us (98%)
    pallas_call x1, Pallas kernels, shards(): pl.pallas_call(kernel, out_shape=results + [jax.ShapeDtypeStruct((8, D),...  61.3 us
    pallas_call x1, Pallas kernels, shards(): pl.pallas_call(functools.partial(finish, q_scale=(tokens * q_heads) ** (-...  2.35 us

profile of v2, /device:TPU:1, one launch (start us, length us, event | category | flops | bytes accessed | tf_op | source)
XLA Modules:
  0.0 64.3 jit_solution(6822675358247700078)
XLA Ops:
  0.6 61.3 %attention.1 = (bf16[1,128,2048]{2,1,0:T(8,128)(2,1)}, bf16[1,128,2048]{2,1,0:T(8,128)(2,1)}, bf16[1,128,1024]{2,1,0:T(8,128)(2,1)}, bf16[1,128,1024]{2,1,0:T(8,128)(2,1)}, f32[8,128]{1,0:T(8,128)}) custom-call(bf16[1,128,2048]{2,1,0:T(8,128)(2,1)} %q_in.1, bf16[1,128,1024]{2,1,0:T(8,128)(2,1)} %k_in.1, bf16[1,128,1024]{2,1,0:T(8,128)(2,1)} %v_in.1, ...), custom_call_target="tpu_custom_call" | custom-call | tf_op jit(solution)/shard_map/attention/pallas_call | solution.py:400
  62.0 2.4 %finish.1 = (bf16[1,128,2048]{2,1,0:T(8,128)(2,1)}, bf16[1,128,2048]{2,1,0:T(8,128)(2,1)}, bf16[1,128,1024]{2,1,0:T(8,128)(2,1)}, bf16[1,128,1024]{2,1,0:T(8,128...) custom-call(bf16[1,128,2048]{2,1,0:T(8,128)(2,1)} %get-tuple-element.17.o_in, bf16[1,128,2048]{2,1,0:T(8,128)(2,1)} %get-tuple-element.18.dq_in, ...), custom_call_target="tpu_custom_call" | custom-call | tf_op jit(solution)/shard_map/finish/pallas_call | solution.py:466

commit v3 on v2

--- a/solution.py
+++ b/solution.py
@@ -13,6 +13,7 @@
 D = 128
 TOK = 128
 SEQ = 16
+DP = 32
 HEADS_KV = 8
 LEN = TOK * SEQ
 B = 256
@@ -59,36 +60,35 @@
     o_out, dq_out, dk_out, dv_out, gain_out,
     q_buf, k_buf, v_aug, g_aug, seg_buf, q_aug, k_aug, k_t, v_t, e_keys, e_queries, ds_keys, q_unit, q_norm,
     o32, o_bf, inv_col, inv_row, g_inv, q_inv, dq_acc, dk_buf, dv_buf, x_k, x_v,
-    gq_bf, gk_bf, gv_bf, qg, kg, part, gain_seq, z_src, z_four, zq_src, z_all,
-    ss, rs, rs_k, rs_v, rs_xk, rs_xv,
+    gq_bf, gk_bf, gv_bf, qg, kg, part, pair, gain_dp, gain_sum, gain_seq,
+    ss, rs, rs_k, rs_v, rs_xk, rs_xv, opened,
 ):
     dp, me = lax.axis_index("dp"), lax.axis_index("seq")
     chip, core = me // 2, me % 2
     sib = me + 1 - 2 * core
-    x_lo, z = dp // 16, dp % 16
     score_scale = D ** (-0.5)
     exponent_scale = score_scale * math.log2(math.e)
 
-    (S_SEG, S_K, S_Q, S_V, S_G, S_KF, S_VF, S_O, S_DQ, S_XK, S_XV, S_DK, S_DV, S_GAIN, S_Z4, S_Z4B, S_ZA, S_Z5, S_QG, S_KG) = range(20)
+    (S_SEG, S_K, S_Q, S_V, S_G, S_KF, S_VF, S_O, S_DQ, S_XK, S_XV, S_DK, S_DV, S_PAIR, S_DP, S_GAIN, S_QG, S_KG) = range(18)
 
     def at_seq(i):
         return (dp, i)
 
-    def at_z(dx, dz):
-        return (((x_lo + dx) % 2) * 16 + (z + dz + 16) % 16, me)
-
-    z_peers = [at_z(0, 4), at_z(0, -4), at_z(0, 1), at_z(0, -1), at_z(0, 2), at_z(0, -2)]
-    z_peers += [at_z(1, 0), at_z(1, 1), at_z(1, -1), at_z(1, 2), at_z(1, -2)]
+    def at_dp(k):
+        return ((dp + k) % DP, me)
 
     barrier = pltpu.get_barrier_semaphore()
 
     def greet(k, _):
-        pl.semaphore_signal(barrier, inc=1, device_id=at_seq((me + k) % SEQ), device_id_type=MESH)
-        return 0
-
-    lax.fori_loop(1, SEQ, greet, 0)
-    for peer in z_peers:
-        pl.semaphore_signal(barrier, inc=1, device_id=peer, device_id_type=MESH)
+        to = 2 * ((chip + k) % NB) + 1
+
+        @pl.when(to != me)
+        def _():
+            pl.semaphore_signal(barrier, inc=1, device_id=at_seq(to), device_id_type=MESH)
+
+        return 0
+
+    lax.fori_loop(0, NB, greet, 0)
 
     lane = lax.broadcasted_iota(jnp.int32, (D, D), 1)
     v_aug[:, D:] = jnp.ones((LEN, D), BF16)
@@ -96,7 +96,15 @@
     pltpu.make_async_copy(qg_in, qg, rs.at[S_QG]).start()
     pltpu.make_async_copy(kg_in, kg, rs.at[S_KG]).start()
 
-    pl.semaphore_wait(barrier, SEQ - 1 + len(z_peers))
+    @pl.when(core == 1)
+    def _():
+        pl.semaphore_wait(barrier, SEQ - 1)
+        pl.semaphore_signal(opened, inc=1, device_id=at_seq(sib), device_id_type=MESH)
+
+    @pl.when(core == 0)
+    def _():
+        pl.semaphore_wait(opened, 1)
+
 
     def remote(src, dst, send, recv, peer):
         pltpu.make_async_remote_copy(src_ref=src, dst_ref=dst, send_sem=send, recv_sem=recv, device_id=peer, device_id_type=MESH).start()
@@ -140,6 +148,14 @@
     send_key_heads(v_in, v_aug.at[mine, pl.ds(0, D)], S_V, rs_v)
     send_heads(q_in, q_buf.at[mine], S_Q)
     send_heads(g_in, g_aug.at[mine, pl.ds(0, D)], S_G)
+
+    @pl.when(core == 0)
+    def _():
+        def greet_dp(k, _):
+            pl.semaphore_signal(barrier, inc=1, device_id=at_dp(k), device_id_type=MESH)
+            return 0
+
+        lax.fori_loop(1, DP, greet_dp, 0)
 
     drain(qg, rs.at[S_QG])
     drain(kg, rs.at[S_KG])
@@ -291,14 +307,25 @@
         slot = pl.ds(j * TOK, TOK)
         remote(dk_buf.at[theirs], x_k.at[slot], ss.at[S_XK], rs_xk.at[j], at_seq(sib))
         remote(dv_buf.at[theirs], x_v.at[slot], ss.at[S_XV], rs_xv.at[j], at_seq(sib))
-    part[...] = gain_part
-
-    def send_gain(k, _):
-        remote(part, gain_seq.at[me], ss.at[S_GAIN], rs.at[S_GAIN], at_seq((me + k) % SEQ))
-        return 0
-
-    lax.fori_loop(1, SEQ, send_gain, 0)
-    gain_seq[me] = part[...]
+
+    part[...] = jnp.sum(gain_part, axis=0, keepdims=True)
+
+    @pl.when(core == 1)
+    def _():
+        remote(part, pair, ss.at[S_PAIR], rs.at[S_PAIR], at_seq(sib))
+
+    @pl.when(core == 0)
+    def _():
+        drain(pair, rs.at[S_PAIR])
+        part[...] += pair[...]
+        pl.semaphore_wait(barrier, DP - 1)
+
+        def send_dp(k, _):
+            remote(part, gain_dp.at[pl.ds(dp, 1)], ss.at[S_DP], rs.at[S_DP], at_dp(k))
+            return 0
+
+        lax.fori_loop(1, DP, send_dp, 0)
+        gain_dp[pl.ds(dp, 1), :] = part[...]
 
     for i in range(NB):
         rows = slice(i * B, (i + 1) * B)
@@ -330,34 +357,34 @@
 
     lax.fori_loop(1, NB, return_keys, 0)
 
-    drain(gain_seq.at[pl.ds(0, SEQ - 1)], rs.at[S_GAIN])
-    trajectory = jnp.sum(gain_seq[...], axis=0)
-    z_src[...] = trajectory
-    four = z // 4
-    z_four[four] = trajectory
-    remote(z_src, z_four.at[four], ss.at[S_Z4], rs.at[S_Z4], at_z(0, 4))
-    remote(z_src, z_four.at[four], ss.at[S_Z4], rs.at[S_Z5], at_z(0, -4))
-    ahead = z_four.at[(four + 1) % 4]
-    drain(ahead, rs.at[S_Z5])
-    remote(ahead, ahead, ss.at[S_Z4B], rs.at[S_Z4B], at_z(0, -4))
-    drain(z_four.at[(four + 3) % 4], rs.at[S_Z4])
-    drain(z_four.at[(four + 2) % 4], rs.at[S_Z4B])
-    column_sum = z_four[0] + z_four[1] + z_four[2] + z_four[3]
-    zq_src[...] = column_sum
-    place = x_lo * 4 + z % 4
-    z_all[place] = column_sum
-    last_peers = [at_z(0, 1), at_z(0, -1), at_z(0, 2), at_z(1, 0), at_z(1, 1), at_z(1, -1), at_z(1, 2)]
-    for peer in last_peers:
-        remote(zq_src, z_all.at[place], ss.at[S_ZA], rs.at[S_ZA], peer)
-    drain(z_all.at[pl.ds(0, 7)], rs.at[S_ZA])
-    total = jnp.sum(jnp.sum(z_all[...], axis=0), axis=0, keepdims=True)
-    gain_out[0:1, :] = total / qg[...]
-    gain_out[1:2, :] = total / kg[...]
+    @pl.when(core == 0)
+    def _():
+        drain(gain_dp.at[pl.ds(0, DP - 1)], rs.at[S_DP])
+        gain_sum[...] = jnp.sum(gain_dp[...], axis=0, keepdims=True)
+
+        def send_gain(k, _):
+            remote(gain_sum, gain_seq.at[pl.ds(chip, 1)], ss.at[S_GAIN], rs.at[S_GAIN], at_seq((me + k) % SEQ))
+            return 0
+
+        lax.fori_loop(1, SEQ, send_gain, 0)
+        gain_seq[pl.ds(chip, 1), :] = gain_sum[...]
 
     drain(o_out.at[0], rs.at[S_O])
     drain(dq_out.at[0], rs.at[S_DQ])
     drain(dk_out.at[0], rs.at[S_DK])
     drain(dv_out.at[0], rs.at[S_DV])
+
+    @pl.when(core == 0)
+    def _():
+        drain(gain_seq.at[pl.ds(0, NB - 1)], rs.at[S_GAIN])
+
+    @pl.when(core == 1)
+    def _():
+        drain(gain_seq, rs.at[S_GAIN])
+
+    total = jnp.sum(gain_seq[...], axis=0, keepdims=True)
+    gain_out[0:1, :] = total / qg[...]
+    gain_out[1:2, :] = total / kg[...]
     most, some = pl.ds(0, LEN - TOK), pl.ds(0, LEN // 2 - TOK)
     drain(seg_buf.at[pl.ds(0, SEQ - 1)], ss.at[S_SEG])
     drain(k_buf.at[some], ss.at[S_K])
@@ -372,10 +399,15 @@
     drain(x_v, ss.at[S_XV])
     drain(gk_bf.at[some], ss.at[S_DK])
     drain(gv_bf.at[some], ss.at[S_DV])
-    drain(gain_seq.at[pl.ds(0, SEQ - 1)], ss.at[S_GAIN])
-    drain(z_four.at[pl.ds(0, 2)], ss.at[S_Z4])
-    drain(z_four.at[0], ss.at[S_Z4B])
-    drain(z_all.at[pl.ds(0, 7)], ss.at[S_ZA])
+
+    @pl.when(core == 1)
+    def _():
+        drain(part, ss.at[S_PAIR])
+
+    @pl.when(core == 0)
+    def _():
+        drain(gain_dp.at[pl.ds(0, DP - 1)], ss.at[S_DP])
+        drain(gain_dp.at[pl.ds(0, SEQ - 1)], ss.at[S_GAIN])
 
 
 def finish(o_in, dq_in, dk_in, dv_in, gains, o_out, dq_out, dk_out, dv_out, q_out, k_out, *, q_scale, k_scale):
@@ -433,18 +465,18 @@
             pltpu.VMEM((LEN // 2, D), BF16),
             pltpu.VMEM((1, D), F32),
             pltpu.VMEM((1, D), F32),
-            pltpu.VMEM((8, D), F32),
-            pltpu.VMEM((SEQ, 8, D), F32),
-            pltpu.VMEM((8, D), F32),
-            pltpu.VMEM((4, 8, D), F32),
-            pltpu.VMEM((8, D), F32),
-            pltpu.VMEM((8, 8, D), F32),
-            dma((20,)),
-            dma((20,)),
+            pltpu.VMEM((1, D), F32),
+            pltpu.VMEM((1, D), F32),
+            pltpu.VMEM((DP, D), F32),
+            pltpu.VMEM((1, D), F32),
+            pltpu.VMEM((NB, D), F32),
+            dma((18,)),
+            dma((18,)),
             dma((8,)),
             dma((8,)),
             dma((8,)),
             dma((8,)),
+            pltpu.SemaphoreType.REGULAR,
         ],
         compiler_params=pltpu.CompilerParams(
             collective_id=0, has_side_effects=True, vmem_limit_bytes=60 << 20

time: 64.8 us -> 60.8 us (0.938)
  Pallas kernels: 63.7 us -> 60.1 us
    pallas_call x1, Pallas kernels: 61.3 us -> 57.7 us  [shards(): pl.pallas_call(kernel, out_shape=results + [jax.ShapeDtypeStruct((8, D),...]
where the time goes in v3:
time: 60.8 us; the launch traced here: 60.7 us
  Pallas kernels  60.1 us (99%)
  between operations  0.64 us (1%)
    pallas_call x1, Pallas kernels, shards(): pl.pallas_call(kernel, out_shape=results + [jax.ShapeDtypeStruct((8, D),...  57.7 us
    pallas_call x1, Pallas kernels, shards(): pl.pallas_call(functools.partial(finish, q_scale=(tokens * q_heads) ** (-...  2.35 us

profile of v3, /device:TPU:1, one launch (start us, length us, event | category | flops | bytes accessed | tf_op | source)
XLA Modules:
  0.0 60.7 jit_solution(6202968370751759485)
XLA Ops:
  0.6 57.7 %attention.1 = (bf16[1,128,2048]{2,1,0:T(8,128)(2,1)}, bf16[1,128,2048]{2,1,0:T(8,128)(2,1)}, bf16[1,128,1024]{2,1,0:T(8,128)(2,1)}, bf16[1,128,1024]{2,1,0:T(8,128)(2,1)}, f32[8,128]{1,0:T(8,128)}) custom-call(bf16[1,128,2048]{2,1,0:T(8,128)(2,1)} %q_in.1, bf16[1,128,1024]{2,1,0:T(8,128)(2,1)} %k_in.1, bf16[1,128,1024]{2,1,0:T(8,128)(2,1)} %v_in.1, ...), custom_call_target="tpu_custom_call" | custom-call | tf_op jit(solution)/shard_map/attention/pallas_call | solution.py:432
  58.3 2.4 %finish.1 = (bf16[1,128,2048]{2,1,0:T(8,128)(2,1)}, bf16[1,128,2048]{2,1,0:T(8,128)(2,1)}, bf16[1,128,1024]{2,1,0:T(8,128)(2,1)}, bf16[1,128,1024]{2,1,0:T(8,128...) custom-call(bf16[1,128,2048]{2,1,0:T(8,128)(2,1)} %get-tuple-element.17.o_in, bf16[1,128,2048]{2,1,0:T(8,128)(2,1)} %get-tuple-element.18.dq_in, ...), custom_call_target="tpu_custom_call" | custom-call | tf_op jit(solution)/shard_map/finish/pallas_call | solution.py:498

commit v4 on v3

--- a/solution.py
+++ b/solution.py
@@ -58,9 +58,9 @@
 def kernel(
     q_in, k_in, v_in, g_in, seg_in, qg_in, kg_in,
     o_out, dq_out, dk_out, dv_out, gain_out,
-    q_buf, k_buf, v_aug, g_aug, seg_buf, q_aug, k_aug, k_t, v_t, e_keys, e_queries, ds_keys, q_unit, q_norm,
-    o32, o_bf, inv_col, inv_row, g_inv, q_inv, dq_acc, dk_buf, dv_buf, x_k, x_v,
-    gq_bf, gk_bf, gv_bf, qg, kg, part, pair, gain_dp, gain_sum, gain_seq,
+    q_buf, k_buf, v_aug, g_aug, seg_buf, q_aug, k_aug, k_t, v_t, e_keys, e_queries, ds_keys, ds_queries, q_unit, q_norm,
+    o32, o_bf, inv_col, inv_row, g_inv, q_inv, dk_buf, dv_buf, x_k, x_v,
+    gq_bf, gk_bf, gv_bf, qg, kg, part, gain_seq, gain_sum, gain_dp,
     ss, rs, rs_k, rs_v, rs_xk, rs_xv, opened,
 ):
     dp, me = lax.axis_index("dp"), lax.axis_index("seq")
@@ -69,13 +69,23 @@
     score_scale = D ** (-0.5)
     exponent_scale = score_scale * math.log2(math.e)
 
-    (S_SEG, S_K, S_Q, S_V, S_G, S_KF, S_VF, S_O, S_DQ, S_XK, S_XV, S_DK, S_DV, S_PAIR, S_DP, S_GAIN, S_QG, S_KG) = range(18)
+    (S_SEG, S_K, S_Q, S_V, S_G, S_KF, S_VF, S_O, S_DQ, S_XK, S_XV, S_DK, S_DV, S_DP, S_GAIN, S_QG, S_KG) = range(17)
 
     def at_seq(i):
         return (dp, i)
 
-    def at_dp(k):
-        return ((dp + k) % DP, me)
+    def at_dp(flip, k):
+        return (((dp // 16 + flip) % 2) * 16 + (dp + k) % 16, me)
+
+    def far_first(act):
+        def both(n, _):
+            k = 8 + ((n + 1) // 2) * (2 * (n % 2) - 1)
+            act(at_dp(0, k))
+            act(at_dp(1, k))
+            return 0
+
+        lax.fori_loop(0, 15, both, 0)
+        act(at_dp(1, 0))
 
     barrier = pltpu.get_barrier_semaphore()
 
@@ -151,11 +161,7 @@
 
     @pl.when(core == 0)
     def _():
-        def greet_dp(k, _):
-            pl.semaphore_signal(barrier, inc=1, device_id=at_dp(k), device_id_type=MESH)
-            return 0
-
-        lax.fori_loop(1, DP, greet_dp, 0)
+        far_first(lambda peer: pl.semaphore_signal(barrier, inc=1, device_id=peer, device_id_type=MESH))
 
     drain(qg, rs.at[S_QG])
     drain(kg, rs.at[S_KG])
@@ -280,111 +286,96 @@
         terms = jnp.where(lanes_b == 0, r1, jnp.where(lanes_b == 1, r2, jnp.where(lanes_b == 2, r3, 0.0)))
         g_aug[rows, D:] = terms.astype(BF16)
 
+    def exchange(j, src, dst, s, sems):
+        theirs = _rows((2 * j + 1 - core) * TOK, TOK)
+        remote(src.at[theirs], dst.at[pl.ds(j * TOK, TOK)], ss.at[s], sems.at[j], at_seq(sib))
+
     gain_part = jnp.zeros((8, D), F32)
     for j in range(NB):
         rows, queries = slice(j * B, (j + 1) * B), slice(j * B, (_blocks(j)[-1] + 1) * B)
-        span = len(_blocks(j)) * B
         v_block = v_aug[rows, :]
         for i in _blocks(j):
             cols = slice((i - j) * B, (i - j + 1) * B)
             gw = lax.dot_general(v_block, g_aug[i * B : (i + 1) * B, :], NT, preferred_element_type=F32)
-            ds_keys[j % 2, :, cols] = (e_keys[rows, cols].astype(F32) * gw).astype(BF16)
-        ds = ds_keys[j % 2, :, :span]
-        dv_buf[rows, :] = _dot(e_keys[rows, :span], g_inv[queries, :])
-        dk = _dot(ds, q_inv[queries, :])
+            ds = (e_keys[rows, cols].astype(F32) * gw).astype(BF16)
+            ds_keys[j % 2, :, cols] = ds
+            at = (i * BAND + j - _first_key(i)) * B
+            ds_queries[at : at + B, :] = ds
+        dk = _dot(ds_keys[j % 2, :, : queries.stop - queries.start], q_inv[queries, :])
         dk_buf[rows, :] = dk
         gain_part = gain_part + _fold(dk * k_aug[rows, :D].astype(F32))
-        part_dq = _dot(k_t[:, rows], ds)
-        if j == 0:
-            dq_acc[:, queries] = part_dq
-        else:
-            old = slice(queries.start, min(queries.stop, (j + BAND - 1) * B))
-            width = old.stop - old.start
-            dq_acc[:, old] += part_dq[:, :width]
-            if width < span:
-                dq_acc[:, old.stop : queries.stop] = part_dq[:, width:]
-        theirs = _rows((2 * j + 1 - core) * TOK, TOK)
-        slot = pl.ds(j * TOK, TOK)
-        remote(dk_buf.at[theirs], x_k.at[slot], ss.at[S_XK], rs_xk.at[j], at_seq(sib))
-        remote(dv_buf.at[theirs], x_v.at[slot], ss.at[S_XV], rs_xv.at[j], at_seq(sib))
+        exchange(j, dk_buf, x_k, S_XK, rs_xk)
 
     part[...] = jnp.sum(gain_part, axis=0, keepdims=True)
 
-    @pl.when(core == 1)
-    def _():
-        remote(part, pair, ss.at[S_PAIR], rs.at[S_PAIR], at_seq(sib))
-
-    @pl.when(core == 0)
-    def _():
-        drain(pair, rs.at[S_PAIR])
-        part[...] += pair[...]
-        pl.semaphore_wait(barrier, DP - 1)
-
-        def send_dp(k, _):
-            remote(part, gain_dp.at[pl.ds(dp, 1)], ss.at[S_DP], rs.at[S_DP], at_dp(k))
+    def send_gain(k, _):
+        remote(part, gain_seq.at[pl.ds(me, 1)], ss.at[S_GAIN], rs.at[S_GAIN], at_seq((me + k) % SEQ))
+        return 0
+
+    lax.fori_loop(1, SEQ, send_gain, 0)
+    gain_seq[pl.ds(me, 1), :] = part[...]
+
+    def return_keys(src, out, s):
+        dst = out.at[0, :, _rows(chip * D, D)]
+        local(src.at[_rows(chip * TOK, TOK)], dst, rs.at[s])
+
+        def one(t, _):
+            j = (chip + t) % NB
+            remote(src.at[_rows(j * TOK, TOK)], dst, ss.at[s], rs.at[s], at_seq(2 * j + core))
             return 0
 
-        lax.fori_loop(1, DP, send_dp, 0)
-        gain_dp[pl.ds(dp, 1), :] = part[...]
-
-    for i in range(NB):
-        rows = slice(i * B, (i + 1) * B)
-        inverse_row = inv_row[i * 8 : (i + 1) * 8, :] * score_scale
-        dq = jnp.transpose((dq_acc[:, rows].reshape(D // 8, 8, B) * inverse_row[None]).reshape(D, B))
-        gq_bf[rows, :] = _norm_backward(dq, q_norm[rows, :], q_unit[rows, :], qg[...]).astype(BF16)
-    return_tiles(gq_bf, dq_out, S_DQ)
+        lax.fori_loop(1, NB, one, 0)
 
     for j in range(NB):
         ours, slot = _rows((2 * j + core) * TOK, TOK), pl.ds(j * TOK, TOK)
         drain(x_k.at[slot], rs_xk.at[j])
-        drain(x_v.at[slot], rs_xv.at[j])
-        gv_bf[slot, :] = (dv_buf[ours, :] + x_v[slot, :]).astype(BF16)
         x = k_buf[ours, :].astype(F32)
         inverse = _inverse_norm(x)
         gk_bf[slot, :] = _norm_backward(dk_buf[ours, :] + x_k[slot, :], inverse, x * inverse, kg[...]).astype(BF16)
 
-    key_cols = _rows(chip * D, D)
-    dk_dst, dv_dst = dk_out.at[0, :, key_cols], dv_out.at[0, :, key_cols]
-    local(gk_bf.at[_rows(chip * TOK, TOK)], dk_dst, rs.at[S_DK])
-    local(gv_bf.at[_rows(chip * TOK, TOK)], dv_dst, rs.at[S_DV])
-
-    def return_keys(t, _):
-        j = (chip + t) % NB
-        slot = _rows(j * TOK, TOK)
-        remote(gk_bf.at[slot], dk_dst, ss.at[S_DK], rs.at[S_DK], at_seq(2 * j + core))
-        remote(gv_bf.at[slot], dv_dst, ss.at[S_DV], rs.at[S_DV], at_seq(2 * j + core))
-        return 0
-
-    lax.fori_loop(1, NB, return_keys, 0)
+    return_keys(gk_bf, dk_out, S_DK)
+
+    for i in range(NB):
+        first, rows = _first_key(i), slice(i * B, (i + 1) * B)
+        keys = (i + 1 - first) * B
+        dq_t = _dot(k_t[:, first * B : (i + 1) * B], ds_queries[i * BAND * B : i * BAND * B + keys, :])
+        inverse_row = inv_row[i * 8 : (i + 1) * 8, :] * score_scale
+        dq = jnp.transpose((dq_t.reshape(D // 8, 8, B) * inverse_row[None]).reshape(D, B))
+        gq_bf[rows, :] = _norm_backward(dq, q_norm[rows, :], q_unit[rows, :], qg[...]).astype(BF16)
+    return_tiles(gq_bf, dq_out, S_DQ)
+
+    drain(gain_seq.at[pl.ds(0, SEQ - 1)], rs.at[S_GAIN])
+    gain_sum[...] = jnp.sum(gain_seq[...], axis=0, keepdims=True)
 
     @pl.when(core == 0)
     def _():
-        drain(gain_dp.at[pl.ds(0, DP - 1)], rs.at[S_DP])
-        gain_sum[...] = jnp.sum(gain_dp[...], axis=0, keepdims=True)
-
-        def send_gain(k, _):
-            remote(gain_sum, gain_seq.at[pl.ds(chip, 1)], ss.at[S_GAIN], rs.at[S_GAIN], at_seq((me + k) % SEQ))
-            return 0
-
-        lax.fori_loop(1, SEQ, send_gain, 0)
-        gain_seq[pl.ds(chip, 1), :] = gain_sum[...]
+        pl.semaphore_wait(barrier, DP - 1)
+        pl.semaphore_signal(opened, inc=1, device_id=at_seq(sib), device_id_type=MESH)
+
+    @pl.when(core == 1)
+    def _():
+        pl.semaphore_wait(opened, 1)
+
+    far_first(lambda peer: remote(gain_sum, gain_dp.at[pl.ds(dp, 1)], ss.at[S_DP], rs.at[S_DP], peer))
+    gain_dp[pl.ds(dp, 1), :] = gain_sum[...]
+    for j in range(NB):
+        rows, queries = slice(j * B, (j + 1) * B), slice(j * B, (_blocks(j)[-1] + 1) * B)
+        dv_buf[rows, :] = _dot(e_keys[rows, : queries.stop - queries.start], g_inv[queries, :])
+        exchange(j, dv_buf, x_v, S_XV, rs_xv)
+
+
+    for j in range(NB):
+        ours, slot = _rows((2 * j + core) * TOK, TOK), pl.ds(j * TOK, TOK)
+        drain(x_v.at[slot], rs_xv.at[j])
+        gv_bf[slot, :] = (dv_buf[ours, :] + x_v[slot, :]).astype(BF16)
+
+    return_keys(gv_bf, dv_out, S_DV)
 
     drain(o_out.at[0], rs.at[S_O])
     drain(dq_out.at[0], rs.at[S_DQ])
     drain(dk_out.at[0], rs.at[S_DK])
     drain(dv_out.at[0], rs.at[S_DV])
 
-    @pl.when(core == 0)
-    def _():
-        drain(gain_seq.at[pl.ds(0, NB - 1)], rs.at[S_GAIN])
-
-    @pl.when(core == 1)
-    def _():
-        drain(gain_seq, rs.at[S_GAIN])
-
-    total = jnp.sum(gain_seq[...], axis=0, keepdims=True)
-    gain_out[0:1, :] = total / qg[...]
-    gain_out[1:2, :] = total / kg[...]
     most, some = pl.ds(0, LEN - TOK), pl.ds(0, LEN // 2 - TOK)
     drain(seg_buf.at[pl.ds(0, SEQ - 1)], ss.at[S_SEG])
     drain(k_buf.at[some], ss.at[S_K])
@@ -400,14 +391,13 @@
     drain(gk_bf.at[some], ss.at[S_DK])
     drain(gv_bf.at[some], ss.at[S_DV])
 
-    @pl.when(core == 1)
-    def _():
-        drain(part, ss.at[S_PAIR])
-
-    @pl.when(core == 0)
-    def _():
-        drain(gain_dp.at[pl.ds(0, DP - 1)], ss.at[S_DP])
-        drain(gain_dp.at[pl.ds(0, SEQ - 1)], ss.at[S_GAIN])
+    drain(gain_dp.at[pl.ds(0, DP - 1)], ss.at[S_DP])
+    drain(gain_seq.at[pl.ds(0, SEQ - 1)], ss.at[S_GAIN])
+
+    drain(gain_dp.at[pl.ds(0, DP - 1)], rs.at[S_DP])
+    total = jnp.sum(gain_dp[...], axis=0, keepdims=True)
+    gain_out[0:1, :] = total / qg[...]
+    gain_out[1:2, :] = total / kg[...]
 
 
 def finish(o_in, dq_in, dk_in, dv_in, gains, o_out, dq_out, dk_out, dv_out, q_out, k_out, *, q_scale, k_scale):
@@ -447,6 +437,7 @@
             pltpu.VMEM((LEN, BAND * B), BF16),
             pltpu.VMEM((NB * BAND * B, B), BF16),
             pltpu.VMEM((2, B, BAND * B), BF16),
+            pltpu.VMEM((NB * BAND * B, B), BF16),
             pltpu.VMEM((LEN, D), F32),
             pltpu.VMEM((LEN, D), F32),
             pltpu.VMEM((LEN, D), F32),
@@ -455,7 +446,6 @@
             pltpu.VMEM((NB * 8, B), F32),
             pltpu.VMEM((LEN, D), BF16),
             pltpu.VMEM((LEN, D), BF16),
-            pltpu.VMEM((D, LEN), F32),
             pltpu.VMEM((LEN, D), F32),
             pltpu.VMEM((LEN, D), F32),
             pltpu.VMEM((LEN // 2, D), F32),
@@ -466,12 +456,11 @@
             pltpu.VMEM((1, D), F32),
             pltpu.VMEM((1, D), F32),
             pltpu.VMEM((1, D), F32),
+            pltpu.VMEM((SEQ, D), F32),
             pltpu.VMEM((1, D), F32),
             pltpu.VMEM((DP, D), F32),
-            pltpu.VMEM((1, D), F32),
-            pltpu.VMEM((NB, D), F32),
-            dma((18,)),
-            dma((18,)),
+            dma((17,)),
+            dma((17,)),
             dma((8,)),
             dma((8,)),
             dma((8,)),

time: 60.8 us -> 57.7 us (0.949)
  Pallas kernels: 60.1 us -> 56.9 us
    pallas_call x1, Pallas kernels: 57.7 us -> 54.5 us  [shards(): pl.pallas_call(kernel, out_shape=results + [jax.ShapeDtypeStruct((8, D),...]
where the time goes in v4:
time: 57.7 us; the launch traced here: 57.5 us
  Pallas kernels  56.9 us (99%)
  between operations  0.64 us (1%)
    pallas_call x1, Pallas kernels, shards(): pl.pallas_call(kernel, out_shape=results + [jax.ShapeDtypeStruct((8, D),...  54.5 us
    pallas_call x1, Pallas kernels, shards(): pl.pallas_call(functools.partial(finish, q_scale=(tokens * q_heads) ** (-...  2.35 us

profile of v4, /device:TPU:1, one launch (start us, length us, event | category | flops | bytes accessed | tf_op | source)
XLA Modules:
  0.0 57.5 jit_solution(5151510565295236708)
XLA Ops:
  0.6 54.5 %attention.1 = (bf16[1,128,2048]{2,1,0:T(8,128)(2,1)}, bf16[1,128,2048]{2,1,0:T(8,128)(2,1)}, bf16[1,128,1024]{2,1,0:T(8,128)(2,1)}, bf16[1,128,1024]{2,1,0:T(8,128)(2,1)}, f32[8,128]{1,0:T(8,128)}) custom-call(bf16[1,128,2048]{2,1,0:T(8,128)(2,1)} %q_in.1, bf16[1,128,1024]{2,1,0:T(8,128)(2,1)} %k_in.1, bf16[1,128,1024]{2,1,0:T(8,128)(2,1)} %v_in.1, ...), custom_call_target="tpu_custom_call" | custom-call | tf_op jit(solution)/shard_map/attention/pallas_call | solution.py:422
  55.2 2.4 %finish.1 = (bf16[1,128,2048]{2,1,0:T(8,128)(2,1)}, bf16[1,128,2048]{2,1,0:T(8,128)(2,1)}, bf16[1,128,1024]{2,1,0:T(8,128)(2,1)}, bf16[1,128,1024]{2,1,0:T(8,128...) custom-call(bf16[1,128,2048]{2,1,0:T(8,128)(2,1)} %get-tuple-element.17.o_in, bf16[1,128,2048]{2,1,0:T(8,128)(2,1)} %get-tuple-element.18.dq_in, ...), custom_call_target="tpu_custom_call" | custom-call | tf_op jit(solution)/shard_map/finish/pallas_call | solution.py:487
